TPU v7x, 256 devices: a whole 4x4x8 slice. The times are simulated.
256 devices in a mesh: dp: 16 (over z_hi, x, core), expert: 16 (over z_lo, y).
Axes of the slice: x: 4, y: 4, z: 8 (z_hi: 2, z_lo: 4; z = z_hi * 4 + z_lo), core: 2. Of those that a mesh axis runs over, the one named last changes fastest.
Arguments:
- patches: bfloat16 [32, 256, 2048], P('dp', None, 'expert'), may hold values from -6 to 6
- visible: int32 [32, 64], P('dp'), may hold values from 0 to 255, as said below
- modality: int32 [32, 64], P('dp'), may hold values from 0 to 1, as said below
- dropped: int32 [32], P('dp'), may hold values from 0 to 2
- attn_gain: float32 [2048], replicated, may hold values from 0.1 to 1.9
- w_qkv: bfloat16 [2048, 3, 2048], P(None, None, 'expert')
- w_out: bfloat16 [2048, 2048], P('expert'), may hold values from -0.125 to 0.125
- ffn_gain: float32 [2048], replicated, may hold values from 0.1 to 1.9
- w_gate: bfloat16 [16, 2048, 4096], P('expert', None, 'dp'), as said below
- w_up: bfloat16 [16, 2048, 4096], P('expert', None, 'dp'), as said below
- w_down: bfloat16 [16, 4096, 2048], P('expert', 'dp'), as said below
- cotangent: bfloat16 [2048, 2048], P(('dp', 'expert')), may hold values from -6 to 6
Outputs:
- output: bfloat16 [2048, 2048], P(('dp', 'expert'))
- grad_qkv: float32 [2048, 3, 2048], P(None, None, 'expert')
- grad_out: float32 [2048, 2048], P('expert')
Inputs may be any that keep to these rules, and one draw needn't show every extreme that they name: `visible`: the 64 indices of each sample are distinct. `modality`: each sample has exactly 16 tokens of value 1. w_gate[e] equals w_gate[e % 2] for e < 12 and w_gate[12 + (e - 12) % 2] otherwise. w_up[e] equals w_up[e % 2] for e < 12 and w_up[12 + (e - 12) % 2] otherwise. w_down[e] equals w_down[e % 2] for e < 12 and w_down[12 + (e - 12) % 2] otherwise.
All inputs are finite; a program needn't handle non-finite values.
Results may differ from a plain program's by a relative error of at most 0.03.
The roundings to bfloat16 on the way count: a program that leaves them out, or rounds other values in their place, can miss the bound.
Values may be sent and summed in bfloat16 or wider, within the bound.
A program may use at most 64 MiB of HBM per device.

v0:
```python
import math

import jax
import jax.numpy as jnp
from jax import lax
from jax.sharding import PartitionSpec as P

HEAD_DIM = 128


def rms_scale(values, gain):
    mean_sq = jnp.mean(values * values, axis=-1, keepdims=True)
    return values * lax.rsqrt(mean_sq + 1e-06) * gain


def attend(queries, key_heads, value_heads, alive_grid):
    factor = 1.0 / math.sqrt(queries.shape[-1])
    scores = (
        jnp.einsum("shqe,shke->shqk", queries, key_heads, preferred_element_type=jnp.float32)
        * factor
    )
    scores = jnp.where(alive_grid[:, None, None, :], scores, -1e30)
    row_top = lax.stop_gradient(jnp.max(scores, axis=-1, keepdims=True))
    weights = jnp.exp(scores - row_top)
    probs = (weights / jnp.sum(weights, axis=-1, keepdims=True)).astype(jnp.bfloat16)
    return jnp.einsum("shqk,shke->shqe", probs, value_heads, preferred_element_type=jnp.float32)


def contract_last(left, right):
    return lax.dot_general(
        left, right, (((1,), (1,)), ((), ())), preferred_element_type=jnp.float32
    )


def contract_first(left, right):
    return lax.dot_general(
        left, right, (((0,), (0,)), ((), ())), preferred_element_type=jnp.float32
    )


def collect_rows(flat_rows, target):
    taken = jnp.take(flat_rows, jnp.maximum(target, 0), axis=0)
    return jnp.sum(jnp.where((target >= 0)[..., None], taken, 0.0), axis=1)


def column_ffn(tok_in, grad_in, gate_local, up_local, down_local):
    gate_acts = jnp.dot(tok_in, gate_local, preferred_element_type=jnp.float32)
    up_acts = jnp.dot(tok_in, up_local, preferred_element_type=jnp.float32)
    logistic = jax.nn.sigmoid(gate_acts)
    active = gate_acts * logistic
    hidden = (active * up_acts).astype(jnp.bfloat16)
    out_part = jnp.dot(hidden, down_local, preferred_element_type=jnp.float32)
    grad_hidden = contract_last(grad_in, down_local)
    grad_gate = (grad_hidden * up_acts * logistic * (1.0 + gate_acts * (1.0 - logistic))).astype(
        jnp.bfloat16
    )
    grad_up = (grad_hidden * active).astype(jnp.bfloat16)
    back_part = contract_last(grad_gate, gate_local) + contract_last(grad_up, up_local)
    return (out_part, back_part)


def route_slots(kind_rows, live_rows, column_idx, column_count):
    split_count = column_count // 8
    opt_count = 3 * column_count // 4
    is_sar = jnp.logical_and(kind_rows == 1, live_rows)
    is_opt = jnp.logical_and(kind_rows == 0, live_rows)
    rank_sar = jnp.cumsum(is_sar.astype(jnp.int32), axis=-1) - 1
    rank_opt = jnp.cumsum(is_opt.astype(jnp.int32), axis=-1) - 1
    rank_all = jnp.where(is_sar, rank_sar, rank_opt)
    copy_count = jnp.where(
        is_sar, (column_count - opt_count) // split_count, opt_count // split_count
    )
    replica = (column_idx + rank_all) % copy_count
    slot_pos = rank_all // copy_count
    first_col = jnp.where(is_sar, opt_count, 0) + replica * split_count
    dest_cols = first_col[..., None] + jnp.arange(split_count, dtype=jnp.int32)
    return (dest_cols, slot_pos)


def body(
    patches,
    visible,
    modality,
    dropped,
    attn_gain,
    w_qkv,
    w_out,
    ffn_gain,
    w_gate,
    w_up,
    w_down,
    cotangent,
):
    sample_count, visible_count = visible.shape
    model_width = w_qkv.shape[0]
    local_width = w_qkv.shape[2]
    local_heads = local_width // HEAD_DIM
    row_total = sample_count * visible_count
    picked = jnp.take_along_axis(patches, visible[:, :, None], axis=1)
    gathered = lax.all_gather(picked, "expert", axis=2, tiled=True)
    tok_rows = gathered.reshape(row_total, model_width)
    alive_grid = jnp.logical_or(dropped[:, None] == 0, modality != dropped[:, None] - 1)
    normed = rms_scale(tok_rows.astype(jnp.float32), attn_gain).astype(jnp.bfloat16)
    projected = jnp.dot(
        normed, w_qkv.reshape(model_width, 3 * local_width), preferred_element_type=jnp.float32
    ).astype(jnp.bfloat16)
    projected = projected.reshape(sample_count, visible_count, 3, local_heads, HEAD_DIM)
    queries = projected[:, :, 0].transpose(0, 2, 1, 3)
    key_heads = projected[:, :, 1].transpose(0, 2, 1, 3)
    value_heads = projected[:, :, 2].transpose(0, 2, 1, 3)
    attended, pullback = jax.vjp(
        lambda q_part, k_part, v_part: attend(q_part, k_part, v_part, alive_grid),
        queries,
        key_heads,
        value_heads,
    )
    head_out = attended.astype(jnp.bfloat16).transpose(0, 2, 1, 3).reshape(row_total, local_width)
    column_count = lax.axis_size("expert")
    own_rows = row_total // column_count
    attn_sum = lax.psum_scatter(
        jnp.dot(head_out, w_out, preferred_element_type=jnp.float32).astype(jnp.bfloat16),
        "expert",
        scatter_dimension=0,
        tiled=True,
    ).astype(jnp.float32)
    column_idx = lax.axis_index("expert")
    row_start = column_idx * own_rows
    residual = (
        lax.dynamic_slice_in_dim(tok_rows, row_start, own_rows, 0).astype(jnp.float32) + attn_sum
    )
    normed_res, norm_back = jax.vjp(lambda values: rms_scale(values, ffn_gain), residual)
    token_bf = normed_res.astype(jnp.bfloat16)
    kind_rows = lax.dynamic_slice_in_dim(modality.reshape(row_total), row_start, own_rows, 0)
    live_rows = lax.dynamic_slice_in_dim(alive_grid.reshape(row_total), row_start, own_rows, 0)
    capacity = own_rows // 2
    gate_local = w_gate[0]
    up_local = w_up[0]
    down_local = w_down[0]
    dest_cols, slot_pos = route_slots(kind_rows, live_rows, column_idx, column_count)
    target = jnp.where(live_rows[:, None], dest_cols * capacity + slot_pos[:, None], -1)
    slot_ids = jnp.arange(column_count * capacity, dtype=jnp.int32)
    slot_hits = jnp.any(target[:, :, None] == slot_ids, axis=1)
    hits_bf = slot_hits.astype(jnp.bfloat16)
    sent_tokens = (
        jnp.einsum("ts,td->sd", hits_bf, token_bf, preferred_element_type=jnp.float32)
        .astype(jnp.bfloat16)
        .reshape(column_count, capacity, model_width)
    )
    sent_grads = (
        jnp.einsum("ts,td->sd", hits_bf, cotangent, preferred_element_type=jnp.float32)
        .astype(jnp.bfloat16)
        .reshape(column_count, capacity, model_width)
    )
    tok_in = lax.all_to_all(sent_tokens, "expert", split_axis=0, concat_axis=0, tiled=True)
    grad_in = lax.all_to_all(sent_grads, "expert", split_axis=0, concat_axis=0, tiled=True)
    tok_all = lax.all_gather(tok_in, "dp", axis=0, tiled=True)
    grad_all = lax.all_gather(grad_in, "dp", axis=0, tiled=True)
    full_shape = tok_all.shape
    out_part, back_part = column_ffn(
        tok_all.reshape(-1, model_width),
        grad_all.reshape(-1, model_width),
        gate_local,
        up_local,
        down_local,
    )
    out_sum = lax.psum_scatter(
        out_part.reshape(full_shape).astype(jnp.bfloat16), "dp", scatter_dimension=0, tiled=True
    ).astype(jnp.float32)
    back_sum = lax.psum_scatter(
        back_part.reshape(full_shape).astype(jnp.bfloat16), "dp", scatter_dimension=0, tiled=True
    ).astype(jnp.float32)
    out_back = lax.all_to_all(
        out_sum.astype(jnp.bfloat16), "expert", split_axis=0, concat_axis=0, tiled=True
    ).astype(out_sum.dtype)
    grad_back = lax.all_to_all(
        back_sum.astype(jnp.bfloat16), "expert", split_axis=0, concat_axis=0, tiled=True
    ).astype(back_sum.dtype)
    expert_out = collect_rows(out_back.reshape(-1, model_width), target)
    grad_in_rows = collect_rows(grad_back.reshape(-1, model_width), target)
    output = (residual + expert_out).astype(jnp.bfloat16)
    grad_resid = (cotangent.astype(jnp.float32) + norm_back(grad_in_rows)[0]).astype(jnp.bfloat16)
    grad_full = lax.all_gather(grad_resid, "expert", axis=0, tiled=True)
    grad_out_part = contract_first(head_out, grad_full)
    grad_heads = contract_last(grad_full, w_out)
    grad_attended = grad_heads.reshape(
        sample_count, visible_count, local_heads, HEAD_DIM
    ).transpose(0, 2, 1, 3)
    grad_query, grad_keys, grad_values = pullback(grad_attended)
    stacked = jnp.stack(
        [grad_part.transpose(0, 2, 1, 3) for grad_part in (grad_query, grad_keys, grad_values)],
        axis=2,
    )
    stacked = stacked.reshape(row_total, 3 * local_width)
    grad_qkv_part = contract_first(normed, stacked).reshape(model_width, 3, local_width)
    grad_qkv, grad_out = (
        lax.psum(grad_qkv_part.astype(jnp.bfloat16), "dp").astype(jnp.float32),
        lax.psum(grad_out_part.astype(jnp.bfloat16), "dp").astype(jnp.float32),
    )
    return (output, grad_qkv, grad_out)


def solution(mesh):
    placed = (
        P("dp", None, "expert"),
        P("dp", None),
        P("dp", None),
        P("dp"),
        P(),
        P(None, None, "expert"),
        P("expert", None),
        P(),
        P("expert", None, "dp"),
        P("expert", None, "dp"),
        P("expert", "dp", None),
        P(("dp", "expert"), None),
    )
    return jax.shard_map(
        body,
        mesh=mesh,
        in_specs=placed,
        out_specs=(P(("dp", "expert"), None), P(None, None, "expert"), P("expert", None)),
        check_vma=False,
    )
```

profile of v0, /device:TPU:1, one launch (start us, length us, event | category | flops | bytes accessed | tf_op | source)
XLA Modules:
  0.0 847.4 jit_solution(11438111626989495694)
XLA Ops:
  8.1 0.7 broadcast_add_fusion
  8.8 0.7 broadcast_compare_fusion.1
  9.5 0.7 compare_and_fusion.1
  10.1 0.7 bitcast_or_fusion
  10.9 2.0 gather_fusion
  13.1 40.7 %all_gather.12 = bf16[2,64,2048]{2,1,0:T(8,128)(2,1)S(1)} all-gather(bf16[2,64,128]{2,1,0:T(8,128)(2,1)S(1)} %broadcast_select_fusion), channel_id=1, replica_groups=mesh['dp'=16,'expert'=16] {'expert'}, dimensions={2}, use_global_device_ids=true | all-gather | bytes 557056 | tf_op jit(solution)/shard_map/all_gather | solution.py:100
  53.9 1.7 copy.44
  55.9 0.8 copy-done.1
  58.0 2.1 convolution_convert_fusion.3
  61.7 12.1 %all_to_all.20 = bf16[16,4,2048]{2,1,0:T(4,128)(2,1)} all-to-all(bf16[16,4,2048]{2,1,0:T(4,128)(2,1)S(1)} %reshape.380), channel_id=1, replica_groups=mesh['dp'=16,'expert'=16] {'expert'}, dimensions={0} | all-to-all | bytes 524288 | tf_op jit(solution)/shard_map/all_to_all | solution.py:155
  73.9 80.3 %reduce-scatter.3.cloned.1.call-done = bf16[8,2048]{1,0:T(8,128)(2,1)} async-done(((bf16[128,2048]{1,0:T(8,128)(2,1)}), bf16[8,2048]{1,0:T(8,128)(2,1)}) %reduce-scatter.3.cloned.1.call-update) | async-done | bytes 32784 | tf_op jit(solution)/shard_map/reduce_scatter | solution.py:120
  154.1 0.9 multiply_reduce_fusion.2
  155.1 1.1 convolution_convert_fusion.5
  156.2 13.6 %all_to_all.21 = bf16[16,4,2048]{2,1,0:T(4,128)(2,1)} all-to-all(bf16[16,4,2048]{2,1,0:T(4,128)(2,1)S(1)} %reshape.376), channel_id=1, replica_groups=mesh['dp'=16,'expert'=16] {'expert'}, dimensions={0} | all-to-all | bytes 524288 | tf_op jit(solution)/shard_map/all_to_all | solution.py:154
  170.0 6.9 reshape.381
  176.9 3.8 fusion.12
  180.7 80.7 %all-gather.3.cloned.1.call-done = bf16[256,4,2048]{2,1,0:T(4,128)(2,1)} async-done(((bf16[16,4,2048]{2,1,0:T(4,128)(2,1)}), bf16[256,4,2048]{2,1,0:T(4,128)(2,1)}) %all-gather.3.cloned.1.call-update) | async-done | bytes 4194320 | tf_op jit(solution)/shard_map/all_gather | solution.py:156
  261.4 7.0 reshape.377
  268.3 3.9 fusion.19
  272.3 2.1 multiply_convert_fusion.2
  274.4 1.6 fusion.17
  275.9 3.4 add_convert_fusion
  279.3 7.2 convert_element_type.134
  286.8 1.2 dot_general.70
  288.0 3.2 convolution_convert_fusion
  292.5 182.0 %all-reduce.5.cloned.1.call-done = bf16[256,4,2048]{2,1,0:T(4,128)(2,1)} async-done(((bf16[256,4,2048]{2,1,0:T(4,128)(2,1)}), bf16[256,4,2048]{2,1,0:T(4,128)(2,1)}) %all-reduce.5.cloned.1.call-update) | async-done | bytes 4194320
  474.5 1.8 constant_dynamic-slice_fusion
  476.3 5.6 all-to-all-start.3
  482.0 100.7 %reduce-scatter.5.cloned.1.call-done = bf16[16,4,2048]{2,0,1:T(8,128)(2,1)} async-done(((bf16[256,4,2048]{2,0,1:T(8,128)(2,1)}), bf16[16,4,2048]{2,0,1:T(8,128)(2,1)}) %reduce-scatter.5.cloned.1.call-update) | async-done | bytes 262160 | tf_op jit(solution)/shard_map/reduce_scatter | solution.py:166
  582.7 1.9 copy.51
  584.5 5.3 all-to-all-start.1
  590.5 0.6 fusion.34
  591.2 0.6 gather_fusion.2
  591.9 6.8 all-to-all-done.1
  599.5 1.1 fusion.25
  600.6 0.9 multiply_reduce_fusion.1
  601.5 0.6 multiply_multiply_fusion
  602.1 1.4 fusion.28
  603.5 35.3 %all_gather.15 = bf16[128,2048]{1,0:T(8,128)(2,1)S(1)} all-gather(bf16[8,2048]{1,0:T(8,128)(2,1)S(1)} %get-tuple-element.11), channel_id=1, replica_groups=mesh['dp'=16,'expert'=16] {'expert'}, dimensions={0}, use_global_device_ids=true | all-gather | bytes 557056 | tf_op jit(solution)/shard_map/all_gather | solution.py:182
  639.1 1.9 convolution_convert_fusion.2
  641.0 1.0 multiply_reduce_fusion
  642.1 1.1 fusion.6
  643.2 0.9 fusion.5
  644.1 0.8 fusion.7
  645.2 1.8 convolution_convert_fusion.1
  647.0 187.4 %all-reduce.7.cloned.1.call-done = (bf16[2048,3,128]{2,0,1:T(8,128)(2,1)}, bf16[128,2048]{1,0:T(8,128)(2,1)}) async-done(((bf16[2048,3,128]{2,0,1:T(8,128)(2,1)}, bf16[128,2048]{1,0:T(8,128)(2,1)}), (bf16[2048,3,128]{2,0,1:T(8,128)(2,1)}, bf16[128,2048]{1,0:T(8,128)(2,1)})) %all-reduce.7.cloned.1.call-update) | async-done | bytes 2097168 | tf_op jit(solution)/shard_map/psum | solution.py:196
  834.4 2.1 convert_element_type.146
  836.5 3.3 convert_element_type.144
  (99 shorter events, 6.7 us)
Async XLA Ops:
  8.0 264.2 %copy-start = (bf16[1,2048,256]{2,1,0:T(8,128)(2,1)S(1)}, bf16[1,2048,256]{2,1,0:T(8,128)(2,1)}, u32[]{:S(2)}) copy-start(bf16[1,2048,256]{2,1,0:T(8,128)(2,1)} %param.23) | copy-start | bytes 3145732
  8.0 47.6 %copy-start.16 = (f32[2048]{0:T(1024)S(1)}, f32[2048]{0:T(1024)}, u32[]{:S(2)}) copy-start(f32[2048]{0:T(1024)} %param.18) | copy-start | bytes 24580
  8.0 146.1 %reduce-scatter.3.cloned.1.call-start = ((), (), s32[]{:S(2)}) async-start(), calls=%async_computation.6 | async-start | bytes 557056 | tf_op jit(solution)/shard_map/reduce_scatter | solution.py:120
  10.9 46.5 %copy-start.18 = (s32[2,64]{1,0:T(2,128)S(1)}, s32[2,64]{1,0:T(2,128)}, u32[]{:S(2)}) copy-start(s32[2,64]{1,0:T(2,128)} %param.16) | copy-start | bytes 1540
  53.9 7.4 copy-start.8
  55.7 99.4 %copy-start.10 = (f32[2048]{0:T(1024)S(1)}, f32[2048]{0:T(1024)}, u32[]{:S(2)}) copy-start(f32[2048]{0:T(1024)} %param.21) | copy-start | bytes 24580
  55.9 0.8 copy-start.1
  57.5 3.8 copy-start.7
  57.5 119.4 %copy-start.13 = (bf16[2,64,1,1,128]{4,2,1,0,3:T(2,128)(2,1)}, bf16[2,64,1,1,128]{4,2,1,0,3:T(2,128)(2,1)S(1)}, u32[]{:S(2)}) copy-start(bf16[2,64,1,1,128]{4,2,1,0,3:T(2,128)(2,1)S(1)} %get-tuple-element.13) | copy-start | bytes 98308
  57.5 119.4 %copy-start.15 = (bf16[2,64,1,1,128]{4,2,1,0,3:T(2,128)(2,1)}, bf16[2,64,1,1,128]{4,2,1,0,3:T(2,128)(2,1)S(1)}, u32[]{:S(2)}) copy-start(bf16[2,64,1,1,128]{4,2,1,0,3:T(2,128)(2,1)S(1)} %get-tuple-element.14) | copy-start | bytes 98308
  57.6 3.3 copy-start.21
  57.8 3.5 copy-start.11
  57.8 532.2 %copy-start.19 = (f32[2,64]{1,0:T(2,128)}, f32[2,64]{1,0:T(2,128)S(1)}, u32[]{:S(2)}) copy-start(f32[2,64]{1,0:T(2,128)S(1)} %get-tuple-element.22) | copy-start | bytes 1540
  58.0 3.3 copy-start.9
  60.1 109.8 %all-gather.5.cloned.1.call-start = ((), (), s32[]{:S(2)}) async-start(), calls=%async_computation.9 | async-start | bytes 4456448 | tf_op jit(solution)/shard_map/all_gather | solution.py:157
  73.8 187.5 %all-gather.3.cloned.1.call-start = ((), (), s32[]{:S(2)}) async-start(), calls=%async_computation.7 | async-start | bytes 4456448 | tf_op jit(solution)/shard_map/all_gather | solution.py:156
  155.0 21.9 %copy-start.20 = (f32[8]{0:T(128)}, f32[8]{0:T(128)S(1)}, u32[]{:S(2)}) copy-start(f32[8]{0:T(128)S(1)} %multiply_reduce_fusion.2) | copy-start | bytes 100
  155.0 21.8 %copy-start.17 = (f32[8]{0:T(128)}, f32[8]{0:T(128)S(1)}, u32[]{:S(2)}) copy-start(f32[8]{0:T(128)S(1)} %fusion.37) | copy-start | bytes 100
  169.9 304.7 %all-reduce.5.cloned.1.call-start = ((), (), s32[]{:S(2)}) async-start(), calls=%async_computation.10 | async-start | bytes 8388608
  268.3 3.9 copy-start.3
  272.2 2.1 copy-start.5
  286.5 1.5 copy-start.6
  286.5 296.2 %reduce-scatter.5.cloned.1.call-start = ((), (), s32[]{:S(2)}) async-start(), calls=%async_computation.8 | async-start | bytes 4456448 | tf_op jit(solution)/shard_map/reduce_scatter | solution.py:166
  288.0 3.3 copy-start.22
  291.2 347.6 %copy-start.4 = (bf16[128,2048]{1,0:T(8,128)(2,1)S(1)}, bf16[128,2048]{1,0:T(8,128)(2,1)}, u32[]{:S(2)}) copy-start(bf16[128,2048]{1,0:T(8,128)(2,1)} %param.20) | copy-start | bytes 1572868
  476.3 108.2 %all-to-all-start.3 = ((bf16[16,4,2048]{2,1,0:T(4,128)(2,1)}), bf16[16,4,2048]{2,1,0:T(4,128)(2,1)S(1)}, u32[]{:S(2)}, u32[]{:S(2)}) async-start(bf16[16,4,2048]{2,1,0:T(4,128)(2,1)} %constant_dynamic-slice_fusion), calls=%async_computation.5 | async-start | bytes 524288 | tf_op jit(solution)/shard_map/all_to_all | solution.py:175
  584.5 14.2 %all-to-all-start.1 = ((bf16[16,4,2048]{2,1,0:T(4,128)(2,1)}), bf16[16,4,2048]{2,1,0:T(4,128)(2,1)S(1)}, u32[]{:S(2)}, u32[]{:S(2)}) async-start(bf16[16,4,2048]{2,1,0:T(4,128)(2,1)} %copy.51), calls=%async_computation.3 | async-start | bytes 524288 | tf_op jit(solution)/shard_map/all_to_all | solution.py:172
  589.9 244.5 %all-reduce.7.cloned.1.call-start = ((), (), s32[]{:S(2)}) async-start(), calls=%async_computation.11 | async-start | bytes 4194304 | tf_op jit(solution)/shard_map/psum | solution.py:196
  591.8 53.3 %copy-start.2 = (bf16[2,64,2048]{2,1,0:T(8,128)(2,1)S(1)}, bf16[2,64,2048]{2,1,0:T(8,128)(2,1)}, u32[]{:S(2)}) copy-start(bf16[2,64,2048]{2,1,0:T(8,128)(2,1)} %copy-done.1) | copy-start | bytes 1572868
  599.4 43.8 %copy-start.12 = (f32[2,64,64]{1,2,0:T(8,128)S(1)}, f32[2,64,64]{1,2,0:T(8,128)}, u32[]{:S(2)}) copy-start(f32[2,64,64]{1,2,0:T(8,128)} %copy-done.11) | copy-start | bytes 98308
  599.4 43.8 %copy-start.14 = (bf16[2,64,1,1,128]{4,2,1,0,3:T(2,128)(2,1)S(1)}, bf16[2,64,1,1,128]{4,2,1,0,3:T(2,128)(2,1)}, u32[]{:S(2)}) copy-start(bf16[2,64,1,1,128]{4,2,1,0,3:T(2,128)(2,1)} %copy-done.13) | copy-start | bytes 98308
Sparse Core Ops, SparseCore 0:
  60.3 93.8 reduce-scatter.2
Sparse Core Ops, SparseCore 1:
  73.9 82.2 all-gather.4
  170.0 91.3 all-gather.2
  286.6 187.9 all-reduce.4
  479.5 103.1 reduce-scatter.4
  647.0 187.3 all-reduce.6
where the time goes:
time: 849 us; the launch traced here: 847 us
  waiting for transfers between devices  638 us (75%)
  blocking collectives  102 us (12%)
  local copies, waits for them, and re-layouts  33.6 us (4%)
  matrix products  30.1 us (4%)
  between operations  16.8 us (2%)
  other arithmetic  15.8 us (2%)
  starting transfers between devices  11.3 us (1%)
    psum x1, waiting for transfers between devices, body(): lax.psum(grad_qkv_part.astype(jnp.bfloat16), 'dp').astype(jnp.float32)  187 us
    unnamed x7, waiting for transfers between devices  182 us
    reduce_scatter x1, waiting for transfers between devices, body(): lax.psum_scatter(out_part.reshape(full_shape).astype(jnp.bfloat16), 'dp',...  101 us
    all_gather x1, waiting for transfers between devices, body(): tok_all = lax.all_gather(tok_in, 'dp', axis=0, tiled=True)  80.7 us
    reduce_scatter x1, waiting for transfers between devices, body(): lax.psum_scatter(jnp.dot(head_out, w_out, preferred_element_type=jnp.floa...  80.3 us
    all_gather x1, blocking collectives, body(): gathered = lax.all_gather(picked, 'expert', axis=2, tiled=True)  40.7 us
    all_gather x1, blocking collectives, body(): grad_full = lax.all_gather(grad_resid, 'expert', axis=0, tiled=True)  35.3 us
  transfers between devices with their start and end apart: 8, of which 6 were waited for; matrix products, arithmetic and copies ran while one was open for 3% of the time, Pallas kernels for 0%

commit v1 on v0

v1 whole, which is shorter than its diff:
```python
import math

import jax
import jax.numpy as jnp
from jax import lax
from jax.experimental import pallas as pl
from jax.experimental.pallas import tpu as pltpu
from jax.sharding import PartitionSpec as P

BF = jnp.bfloat16
F32 = jnp.float32
MESH = pl.DeviceIdType.MESH
D = 2048
EPS = 1e-06
FACTOR = 1.0 / math.sqrt(128)


def dot(a, b):
    return jnp.dot(a, b, preferred_element_type=F32)


def dot_nt(a, b):
    return lax.dot_general(a, b, (((1,), (1,)), ((), ())), preferred_element_type=F32)


def kernel(
    dropped_ref,
    patches_ref,
    visible_ref,
    modality_ref,
    again_ref,
    fgain_ref,
    cot_ref,
    wqkv_hbm,
    wout_hbm,
    wg_hbm,
    wu_hbm,
    wd_hbm,
    out_ref,
    gfin,
    wqkv,
    wout,
    wg,
    wu,
    wd,
    gath,
    cotg,
    part,
    attr,
    normed,
    norm_t,
    probs32,
    tokg,
    cotr,
    tmat,
    cmat,
    osum,
    r1,
    s1,
    r2,
    s3,
    r3,
    outg,
    grg,
    grmat,
    gbuf,
    h1,
    t1,
    h2,
    t3,
    h3,
    wsem,
    ssem,
    sem_pick,
    sem_cot,
    sem_attn,
    sem_tok,
    sem_cotr,
    sem_d1,
    sem_d2,
    sem_d3,
    sem_gr,
    sem_out,
    sem_g1,
    sem_g2,
    sem_g3,
    sem_fin,
):
    d = lax.axis_index("dp")
    e = lax.axis_index("expert")
    zh = d // 8
    x = (d // 2) % 4
    c = d % 2
    zl = e // 4
    y = e % 4
    h = y % 2
    xh = x * 2 + h
    sib = (zh * 8 + x * 2 + (1 - c), e)
    z_row = (1 - zh) * 8 + x * 2 + c
    zpart = (z_row, ((6 - zl) % 4) * 4 + y)
    zsame = (z_row, e)

    def exp_peer(k):
        q = (e + k) % 16
        return q, (d, q)

    def xh_peer(k):
        q = (xh + k) % 8
        return q, (zh * 8 + (q // 2) * 2 + c, zl * 4 + (y // 2) * 2 + q % 2)

    def x_peer(k):
        q = (x + k) % 4
        return q, (zh * 8 + q * 2 + c, e)

    def send(src, dst, s_sem, r_sem, dev):
        pltpu.make_async_remote_copy(
            src_ref=src, dst_ref=dst, send_sem=s_sem, recv_sem=r_sem,
            device_id=dev, device_id_type=MESH,
        ).start()

    def arrived(dst, r_sem):
        pltpu.make_async_remote_copy(
            src_ref=dst, dst_ref=dst, send_sem=ssem.at[0], recv_sem=r_sem,
            device_id=sib, device_id_type=MESH,
        ).wait_recv()

    def sent(src, s_sem):
        pltpu.make_async_remote_copy(
            src_ref=src, dst_ref=src, send_sem=s_sem, recv_sem=sem_d3.at[0],
            device_id=sib, device_id_type=MESH,
        ).wait_send()

    def loop(lo, hi, fn):
        def step(k, carry):
            fn(k)
            return carry

        lax.fori_loop(lo, hi, step, 0)

    loads = [
        pltpu.make_async_copy(src, dst, wsem.at[i])
        for i, (src, dst) in enumerate(
            ((wqkv_hbm, wqkv), (wout_hbm, wout), (wg_hbm, wg), (wu_hbm, wu), (wd_hbm, wd))
        )
    ]
    for load in loads:
        load.start()

    barrier = pltpu.get_barrier_semaphore()

    def greet(dev):
        pl.semaphore_signal(barrier, inc=1, device_id=dev, device_id_type=MESH)

    loop(1, 16, lambda k: greet(exp_peer(k)[1]))
    loop(1, 8, lambda k: greet(xh_peer(k)[1]))
    greet(sib)
    greet(zpart)
    greet(zsame)

    mod = modality_ref[...].astype(F32)
    upto = (
        lax.broadcasted_iota(jnp.int32, (64, 64), 0) <= lax.broadcasted_iota(jnp.int32, (64, 64), 1)
    ).astype(F32)
    samp_col = lax.broadcasted_iota(jnp.int32, (2, 64), 0).astype(F32)
    rank_sar = dot(mod, upto) - 1.0
    rank_opt = dot(1.0 - mod, upto) - 1.0
    place = jnp.where(mod > 0.5, 96.0 + 16.0 * samp_col + rank_sar, 48.0 * samp_col + rank_opt)
    slot_iota = lax.broadcasted_iota(jnp.int32, (128, 64), 0).astype(F32)
    patch_iota = lax.broadcasted_iota(jnp.int32, (256, 64), 0)
    place_hot = [
        jnp.where(slot_iota == place[s : s + 1, :], 1.0, 0.0).astype(BF) for s in range(2)
    ]
    picked = jnp.zeros((128, 128), F32)
    for s in range(2):
        patch_hot = jnp.where(patch_iota == visible_ref[s : s + 1, :], 1.0, 0.0).astype(BF)
        picked += dot(dot_nt(place_hot[s], patch_hot).astype(BF), patches_ref[s])
    gath[e] = picked.reshape(16, 8, 128).astype(BF)
    cotg[e] = cot_ref[...]

    pl.semaphore_wait(barrier, 25)

    def send_pick(k):
        q, dev = exp_peer(k)
        send(gath.at[e], gath.at[e], ssem.at[0], sem_pick.at[e], dev)

    loop(1, 16, send_pick)

    def send_cot(k):
        q, dev = exp_peer(k)
        send(cotg.at[e], cotg.at[e], ssem.at[1], sem_cot.at[e], dev)

    loop(1, 16, send_cot)

    def wait_pick(k):
        q, dev = exp_peer(k)
        arrived(gath.at[q], sem_pick.at[q])

    loop(1, 16, wait_pick)

    total = jnp.zeros((128, 128), F32)
    for b in range(16):
        xb = gath[b].astype(F32).reshape(128, 128)
        total += xb * xb
    scale = lax.rsqrt(jnp.sum(total, axis=-1, keepdims=True) * (1.0 / D) + EPS)
    for b in range(16):
        xb = gath[b].astype(F32).reshape(128, 128)
        normed[:, b * 128 : (b + 1) * 128] = (xb * scale * again_ref[b : b + 1, :]).astype(BF)
    loads[0].wait()
    q_act, k_act, v_act = (dot(normed[...], wqkv[i]).astype(BF) for i in range(3))
    row_i = lax.broadcasted_iota(jnp.int32, (128, 128), 0)
    col_i = lax.broadcasted_iota(jnp.int32, (128, 128), 1)

    def sample_of(i):
        second = jnp.logical_or(jnp.logical_and(i >= 48, i < 96), i >= 112)
        return jnp.where(second, 1, 0)

    drop0 = dropped_ref[0]
    drop1 = dropped_ref[1]
    col_samp = sample_of(col_i)
    col_drop = jnp.where(col_samp == 1, drop1, drop0)
    col_kind = jnp.where(col_i >= 96, 2, 1)
    keep = jnp.logical_and(sample_of(row_i) == col_samp, col_drop != col_kind)
    scores = jnp.where(keep, dot_nt(q_act, k_act) * FACTOR, -1e30)
    weights = jnp.exp(scores - jnp.max(scores, axis=-1, keepdims=True))
    soft = weights / jnp.sum(weights, axis=-1, keepdims=True)
    probs32[...] = soft
    head_out = dot(soft.astype(BF), v_act).astype(BF)
    loads[1].wait()
    for b in range(4):
        cols = slice(b * 512, (b + 1) * 512)
        part[:, :, cols] = dot(head_out, wout[:, cols]).reshape(16, 8, 512).astype(BF)
    attr[e] = part[e]

    def send_attn(k):
        q, dev = exp_peer(k)
        send(part.at[q], attr.at[e], ssem.at[2], sem_attn.at[e], dev)

    loop(1, 16, send_attn)

    own_slot = ((c * 4 + x) * 2 + h) * 2 + zh

    def slot_of(core, q, z):
        return (core * 8 + q) * 2 + z

    def wait_cot(k):
        q, dev = exp_peer(k)
        arrived(cotg.at[q], sem_cot.at[q])

    loop(1, 16, wait_cot)
    own_iota = (lax.broadcasted_iota(jnp.int32, (8, 64), 0) + e * 8).astype(F32)
    cot_own = jnp.zeros((8, D), F32)
    for s in range(2):
        hot = jnp.where(own_iota == place[s : s + 1, :], 1.0, 0.0).astype(BF)
        rows = cotg[8 * s : 8 * s + 8].astype(F32).reshape(64, D).astype(BF)
        cot_own += dot(hot, rows)
    cotr[own_slot] = cot_own.astype(BF)

    def spread_first(buf, s_sem, r_sem):
        src = buf.at[own_slot]
        send(src, src, s_sem, r_sem.at[own_slot], zpart)

        def step(k):
            send(src, src, s_sem, r_sem.at[own_slot], xh_peer(k)[1])

        loop(1, 8, step)
        send(src, src, s_sem, r_sem.at[own_slot], sib)

    def spread_next(buf, s_sem, r_sem):
        other = slot_of(c, xh, 1 - zh)
        src = buf.at[other]
        arrived(src, r_sem.at[other])

        def step(k):
            send(src, src, s_sem, r_sem.at[other], xh_peer(k)[1])

        loop(1, 8, step)
        send(src, src, s_sem, r_sem.at[other], sib)

    def spread_last(buf, s_sem, r_sem):
        for z in (zh, 1 - zh):

            def step(k):
                slot = slot_of(c, (xh + 8 - k) % 8, z)
                arrived(buf.at[slot], r_sem.at[slot])
                send(buf.at[slot], buf.at[slot], s_sem, r_sem.at[slot], sib)

            loop(1, 8, step)

    def spread_done(buf, r_sem):
        def step(k):
            slot = (1 - c) * 16 + k
            arrived(buf.at[slot], r_sem.at[slot])

        loop(0, 16, step)

    spread_first(cotr, ssem.at[3], sem_cotr)
    for b in range(16):
        cols = slice(b * 128, (b + 1) * 128)
        norm_t[cols, :] = normed[:, cols].astype(F32).T.astype(BF)
    head_t = head_out.astype(F32).T.astype(BF)
    probs_t = soft.T.astype(BF)

    def wait_attn(k):
        q, dev = exp_peer(k)
        arrived(attr.at[q], sem_attn.at[q])

    loop(1, 16, wait_attn)
    own = jnp.concatenate([gath[b, e].astype(F32) for b in range(16)], axis=-1)
    attn_sum = attr[0].astype(F32)
    for b in range(1, 16):
        attn_sum += attr[b].astype(F32)
    residual = own + attn_sum
    res_scale = lax.rsqrt(jnp.mean(residual * residual, axis=-1, keepdims=True) + EPS)
    fgain = fgain_ref[...]
    tokg[own_slot] = (residual * res_scale * fgain).astype(BF)
    spread_first(tokg, ssem.at[4], sem_tok)
    spread_next(cotr, ssem.at[3], sem_cotr)
    spread_next(tokg, ssem.at[4], sem_tok)
    spread_last(cotr, ssem.at[3], sem_cotr)
    spread_last(tokg, ssem.at[4], sem_tok)
    spread_done(cotr, sem_cotr)

    def pack_rows(dst, buf):
        for b in range(8):
            rows = buf[4 * b : 4 * b + 4].astype(F32).reshape(32, D)
            dst[32 * b : 32 * b + 32, :] = rows.astype(BF)

    pack_rows(cmat, cotr)
    loads[2].wait()
    loads[3].wait()
    loads[4].wait()
    grad_hidden = dot_nt(cmat[...], wd[...])
    spread_done(tokg, sem_tok)
    pack_rows(tmat, tokg)
    gate = dot(tmat[...], wg[...])
    up = dot(tmat[...], wu[...])
    logistic = jax.nn.sigmoid(gate)
    active = gate * logistic
    hidden = (active * up).astype(BF)
    grad_gate = (grad_hidden * up * logistic * (1.0 + gate * (1.0 - logistic))).astype(BF)
    grad_up = (grad_hidden * active).astype(BF)
    for b in range(4):
        cols = slice(b * 512, (b + 1) * 512)
        osum[:, 0, :, cols] = dot(hidden, wd[:, cols]).reshape(32, 8, 512).astype(BF)
        back = dot_nt(grad_gate, wg[cols, :]) + dot_nt(grad_up, wu[cols, :])
        osum[:, 1, :, cols] = back.reshape(32, 8, 512).astype(BF)

    def d1_send(k):
        q = (xh + k) % 8
        send(
            osum.at[pl.ds(slot_of(1 - c, q, 0), 2)], r1.at[pl.ds(2 * q, 2)], ssem.at[5],
            sem_d1.at[q], sib,
        )

    loop(1, 9, d1_send)

    def d1_sum(q):
        arrived(r1.at[pl.ds(2 * q, 2)], sem_d1.at[q])
        for z in range(2):
            slot = 2 * q + z
            s1[slot] = (osum[c * 16 + slot].astype(F32) + r1[slot].astype(F32)).astype(BF)

    def d1_step(k):
        q, dev = xh_peer(k)
        d1_sum(q)
        send(s1.at[pl.ds(2 * q, 2)], r2.at[pl.ds(2 * xh, 2)], ssem.at[6], sem_d2.at[xh], dev)

    loop(1, 8, d1_step)
    d1_sum(xh)
    for z in range(2):
        r2[2 * xh + z] = s1[2 * xh + z]

    def wait_d2(k):
        q = (xh + k) % 8
        arrived(r2.at[pl.ds(2 * q, 2)], sem_d2.at[q])

    loop(1, 8, wait_d2)

    def d2_sum(z):
        acc = r2[z].astype(F32)
        for b in range(1, 8):
            acc += r2[2 * b + z].astype(F32)
        return acc

    s3[...] = d2_sum(1 - zh).astype(BF)
    send(s3, r3, ssem.at[7], sem_d3.at[0], zpart)
    sums = d2_sum(zh)
    arrived(r3, sem_d3.at[0])
    own_second = jnp.where(
        jnp.logical_or(jnp.logical_and(e >= 6, e < 12), e >= 14), drop1, drop0
    )
    own_kind = jnp.where(e >= 12, 2, 1)
    alive = jnp.where(own_second != own_kind, 1.0, 0.0)
    sums = (sums + r3[...].astype(F32)) * alive
    grad_in = sums[1] * fgain
    dot_mean = jnp.mean(residual * grad_in, axis=-1, keepdims=True)
    grad_norm = grad_in * res_scale - residual * (res_scale * res_scale * res_scale * dot_mean)
    grg[e] = (cot_own + grad_norm).astype(BF)

    def send_gr(k):
        q, dev = exp_peer(k)
        send(grg.at[e], grg.at[e], ssem.at[8], sem_gr.at[e], dev)

    loop(1, 16, send_gr)
    outg[e] = (residual + sums[0]).astype(BF)

    def send_out(k):
        q, dev = exp_peer(k)
        send(outg.at[e], outg.at[e], ssem.at[9], sem_out.at[e], dev)

    loop(1, 16, send_out)

    def wait_gr(k):
        q, dev = exp_peer(k)
        arrived(grg.at[q], sem_gr.at[q])

    loop(1, 16, wait_gr)

    for b in range(4):
        grmat[32 * b : 32 * b + 32, :] = (
            grg[4 * b : 4 * b + 4].astype(F32).reshape(32, D).astype(BF)
        )
    grad_att = dot_nt(grmat[...], wout[...]).astype(BF)
    soft_b = probs32[...]
    grad_probs = dot_nt(grad_att, v_act).astype(BF).astype(F32)
    grad_v = dot(probs_t, grad_att).astype(BF)
    row_sum = jnp.sum(grad_probs * soft_b, axis=-1, keepdims=True)
    grad_scores = soft_b * (grad_probs - row_sum)
    grad_q = (dot(grad_scores.astype(BF), k_act) * FACTOR).astype(BF)
    grad_k = (dot(grad_scores.T.astype(BF), q_act) * FACTOR).astype(BF)
    stacked = (grad_q, grad_k, grad_v)
    for j in range(12):
        f0 = (j % 4) * 512
        gbuf[j] = dot(norm_t[f0 : f0 + 512, :], stacked[j // 4]).astype(BF)
    for j in range(4):
        for b in range(4):
            c0 = (4 * j + b) * 128
            gbuf[12 + j, b * 128 : (b + 1) * 128, :] = dot(
                head_t, grmat[:, c0 : c0 + 128]
            ).astype(BF)

    def g1_send(k):
        q = (x + k) % 4
        send(
            gbuf.at[pl.ds((1 - c) * 8 + 2 * q, 2)], h1.at[pl.ds(2 * q, 2)], ssem.at[10],
            sem_g1.at[q], sib,
        )

    loop(1, 5, g1_send)

    def g1_sum(q):
        arrived(h1.at[pl.ds(2 * q, 2)], sem_g1.at[q])
        for z in range(2):
            i = 2 * q + z
            t1[i] = (gbuf[c * 8 + i].astype(F32) + h1[i].astype(F32)).astype(BF)

    def g1_step(k):
        q, dev = x_peer(k)
        g1_sum(q)
        send(t1.at[pl.ds(2 * q, 2)], h2.at[pl.ds(2 * x, 2)], ssem.at[11], sem_g2.at[x], dev)

    loop(1, 4, g1_step)
    g1_sum(x)
    for z in range(2):
        h2[2 * x + z] = t1[2 * x + z]

    def wait_g2(k):
        q = (x + k) % 4
        arrived(h2.at[pl.ds(2 * q, 2)], sem_g2.at[q])

    loop(1, 4, wait_g2)

    def g2_sum(z):
        acc = h2[z].astype(F32)
        for b in range(1, 4):
            acc += h2[2 * b + z].astype(F32)
        return acc

    t3[...] = g2_sum(1 - zh).astype(BF)
    send(t3, h3, ssem.at[12], sem_g3.at[0], zsame)
    seg_sum = g2_sum(zh)
    arrived(h3, sem_g3.at[0])
    seg = (c * 4 + x) * 2 + zh
    seg_z = (c * 4 + x) * 2 + 1 - zh
    gfin[seg] = (seg_sum + h3[...].astype(F32)).astype(BF)

    def fin(slot, dev):
        send(gfin.at[slot], gfin.at[slot], ssem.at[13], sem_fin.at[slot], dev)

    fin(seg, zsame)
    loop(1, 4, lambda k: fin(seg, x_peer(k)[1]))
    fin(seg, sib)

    def wait_out(k):
        q, dev = exp_peer(k)
        arrived(outg.at[q], sem_out.at[q])

    loop(1, 16, wait_out)
    row8 = lax.broadcasted_iota(jnp.int32, (8, 64), 0) + e * 8
    col8 = lax.broadcasted_iota(jnp.int32, (8, 64), 1)
    back_hot = jnp.zeros((8, 128), F32)
    for s in range(2):
        back_hot += dot_nt(jnp.where(row8 == col8 + 64 * s, 1.0, 0.0).astype(BF), place_hot[s])
    out_rows = outg[...].astype(F32).reshape(128, D).astype(BF)
    out_ref[...] = dot(back_hot.astype(BF), out_rows).astype(BF)

    arrived(gfin.at[seg_z], sem_fin.at[seg_z])
    loop(1, 4, lambda k: fin(seg_z, x_peer(k)[1]))
    fin(seg_z, sib)
    for z in (zh, 1 - zh):

        def fin_step(k):
            slot = (c * 4 + (x + 4 - k) % 4) * 2 + z
            arrived(gfin.at[slot], sem_fin.at[slot])
            fin(slot, sib)

        loop(1, 4, fin_step)

    def fin_wait(k):
        slot = (1 - c) * 8 + k
        arrived(gfin.at[slot], sem_fin.at[slot])

    loop(0, 8, fin_wait)

    sent(gath.at[pl.ds(0, 15)], ssem.at[0])
    sent(cotg.at[pl.ds(0, 15)], ssem.at[1])
    sent(attr.at[pl.ds(0, 15)], ssem.at[2])
    sent(cotr.at[pl.ds(0, 31)], ssem.at[3])
    sent(tokg.at[pl.ds(0, 31)], ssem.at[4])
    sent(r1, ssem.at[5])
    sent(r2.at[pl.ds(0, 14)], ssem.at[6])
    sent(r3, ssem.at[7])
    sent(grg.at[pl.ds(0, 15)], ssem.at[8])
    sent(outg.at[pl.ds(0, 15)], ssem.at[9])
    sent(h1, ssem.at[10])
    sent(h2.at[pl.ds(0, 6)], ssem.at[11])
    sent(h3, ssem.at[12])
    sent(gfin.at[pl.ds(0, 15)], ssem.at[13])


def layer(patches, visible, modality, dropped, again, w_qkv, w_out, fgain, wg, wu, wd, cot):
    vm = pl.BlockSpec(memory_space=pltpu.VMEM)
    anywhere = pl.BlockSpec(memory_space=pl.ANY)
    dma = pltpu.SemaphoreType.DMA
    scratch = [
        pltpu.VMEM((3, D, 128), BF),
        pltpu.VMEM((128, D), BF),
        pltpu.VMEM((D, 256), BF),
        pltpu.VMEM((D, 256), BF),
        pltpu.VMEM((256, D), BF),
        pltpu.VMEM((16, 16, 8, 128), BF),
        pltpu.VMEM((16, 8, D), BF),
        pltpu.VMEM((16, 8, D), BF),
        pltpu.VMEM((16, 8, D), BF),
        pltpu.VMEM((128, D), BF),
        pltpu.VMEM((D, 128), BF),
        pltpu.VMEM((128, 128), F32),
        pltpu.VMEM((32, 8, D), BF),
        pltpu.VMEM((32, 8, D), BF),
        pltpu.VMEM((256, D), BF),
        pltpu.VMEM((256, D), BF),
        pltpu.VMEM((32, 2, 8, D), BF),
        pltpu.VMEM((16, 2, 8, D), BF),
        pltpu.VMEM((16, 2, 8, D), BF),
        pltpu.VMEM((16, 2, 8, D), BF),
        pltpu.VMEM((2, 8, D), BF),
        pltpu.VMEM((2, 8, D), BF),
        pltpu.VMEM((16, 8, D), BF),
        pltpu.VMEM((16, 8, D), BF),
        pltpu.VMEM((128, D), BF),
        pltpu.VMEM((16, 512, 128), BF),
        pltpu.VMEM((8, 512, 128), BF),
        pltpu.VMEM((8, 512, 128), BF),
        pltpu.VMEM((8, 512, 128), BF),
        pltpu.VMEM((512, 128), BF),
        pltpu.VMEM((512, 128), BF),
        dma((5,)),
        dma((14,)),
        dma((16,)),
        dma((16,)),
        dma((16,)),
        dma((32,)),
        dma((32,)),
        dma((8,)),
        dma((8,)),
        dma((1,)),
        dma((16,)),
        dma((16,)),
        dma((4,)),
        dma((4,)),
        dma((1,)),
        dma((16,)),
    ]
    out, grads = pl.pallas_call(
        kernel,
        out_shape=(
            jax.ShapeDtypeStruct((8, D), BF),
            jax.ShapeDtypeStruct((16, 512, 128), BF),
        ),
        in_specs=[pl.BlockSpec(memory_space=pltpu.SMEM)] + [vm] * 6 + [anywhere] * 5,
        out_specs=(vm, vm),
        scratch_shapes=scratch,
        compiler_params=pltpu.CompilerParams(
            collective_id=0, has_side_effects=True, vmem_limit_bytes=56 * 1024 * 1024
        ),
        name="layer",
    )(
        dropped,
        patches,
        visible,
        modality,
        again.reshape(16, 128),
        fgain.reshape(1, D),
        cot,
        w_qkv.transpose(1, 0, 2),
        w_out,
        wg[0],
        wu[0],
        wd[0],
    )
    grad_qkv = grads[:12].reshape(3, D, 128).transpose(1, 0, 2).astype(F32)
    grad_out = grads[12:].reshape(16, 128, 128).transpose(1, 0, 2).reshape(128, D).astype(F32)
    return out, grad_qkv, grad_out


def solution(mesh):
    placed = (
        P("dp", None, "expert"),
        P("dp", None),
        P("dp", None),
        P("dp"),
        P(),
        P(None, None, "expert"),
        P("expert", None),
        P(),
        P("expert", None, "dp"),
        P("expert", None, "dp"),
        P("expert", "dp", None),
        P(("dp", "expert"), None),
    )
    return jax.shard_map(
        layer,
        mesh=mesh,
        in_specs=placed,
        out_specs=(P(("dp", "expert"), None), P(None, None, "expert"), P("expert", None)),
        check_vma=False,
    )
```

time: 849 us -> 153 us (0.18)
  the two profiles are of different devices: /device:TPU:1 before, /device:TPU:125 now
where the time goes in v1:
time: 153 us
  Pallas kernels  146 us (95%)
  local copies, waits for them, and re-layouts  3.21 us (2%)
  other arithmetic  2.94 us (2%)
    pallas_call x1, Pallas kernels, layer(): pl.pallas_call(kernel, out_shape=(jax.ShapeDtypeStruct((8, D), BF), jax.S...  146 us

profile of v1, /device:TPU:125, one launch (start us, length us, event | category | flops | bytes accessed | tf_op | source)
XLA Modules:
  0.0 152.6 jit_solution(11368284711695689751)
XLA Ops:
  0.6 145.8 %layer.1 = (bf16[8,2048]{1,0:T(8,128)(2,1)}, bf16[16,512,128]{2,1,0:T(8,128)(2,1)}) custom-call(s32[2]{0:T(128)} %dropped_ref.1, bf16[2,256,128]{2,1,0:T(8,128)(2,1)} %patches_ref.1, s32[2,64]{1,0:T(2,128)} %visible_ref.1, s32[2,64]{1,0:T(2,128)} %modality_ref.1, f32[16,128]{1,0:T(8,128)} %bitcast.26, f32[1,2048]{1,0:T(1,128)} %bitcast.27, ...), custom_call_target="tpu_custom_call" | custom-call | tf_op jit(solution)/shard_map/layer/pallas_call | solution.py:594
  146.5 1.1 slice.7
  147.5 1.5 slice.6
  149.1 1.1 copy_bitcast_fusion
  150.1 0.0 copy-start
  150.1 1.9 %convert_bitcast_fusion = f32[2048,3,128]{2,0,1:T(8,128)} fusion(bf16[3,2048,128]{2,1,0:T(8,128)(2,1)S(1)} %bitcast.20), kind=kLoop, calls=%fused_computation | loop fusion | flops 786432 | bytes 4718592 | tf_op jit(solution)/shard_map/convert_element_type | solution.py:621
  152.0 0.0 copy-done
  152.0 0.6 copy.19
Async XLA Ops:
  150.1 1.9 %copy-start = (bf16[8,2048]{1,0:T(8,128)(2,1)S(1)}, bf16[8,2048]{1,0:T(8,128)(2,1)}, u32[]{:S(2)}) copy-start(bf16[8,2048]{1,0:T(8,128)(2,1)} %get-tuple-element.10) | copy-start | bytes 98308

commit v2 on v1

--- a/solution.py
+++ b/solution.py
@@ -37,7 +37,8 @@
     wu_hbm,
     wd_hbm,
     out_ref,
-    gfin,
+    gq_fin,
+    go_fin,
     wqkv,
     wout,
     wg,
@@ -46,7 +47,9 @@
     gath,
     cotg,
     part,
-    attr,
+    party,
+    zsum,
+    partz,
     normed,
     norm_t,
     probs32,
@@ -63,17 +66,24 @@
     outg,
     grg,
     grmat,
-    gbuf,
-    h1,
-    t1,
-    h2,
-    t3,
-    h3,
+    go_part,
+    go_near,
+    go_both,
+    go_ring,
+    go_out,
+    go_in,
+    gq_part,
+    gq_near,
+    gq_both,
+    gq_ring,
+    gq_out,
+    gq_in,
     wsem,
     ssem,
     sem_pick,
     sem_cot,
-    sem_attn,
+    sem_ay,
+    sem_az,
     sem_tok,
     sem_cotr,
     sem_d1,
@@ -84,7 +94,11 @@
     sem_g1,
     sem_g2,
     sem_g3,
-    sem_fin,
+    sem_go,
+    sem_q1,
+    sem_q2,
+    sem_q3,
+    sem_gq,
 ):
     d = lax.axis_index("dp")
     e = lax.axis_index("expert")
@@ -104,6 +118,14 @@
         q = (e + k) % 16
         return q, (d, q)
 
+    def z_peer(k):
+        q = (zl + k) % 4
+        return q, (d, q * 4 + y)
+
+    def y_peer(k):
+        q = (y + k) % 4
+        return q, (d, zl * 4 + q)
+
     def xh_peer(k):
         q = (xh + k) % 8
         return q, (zh * 8 + (q // 2) * 2 + c, zl * 4 + (y // 2) * 2 + q % 2)
@@ -136,6 +158,33 @@
             return carry
 
         lax.fori_loop(lo, hi, step, 0)
+
+    def gather_z(buf, s_sem, r_sem):
+        loop(1, 4, lambda k: send(buf.at[e], buf.at[e], s_sem, r_sem.at[e], z_peer(k)[1]))
+
+    def gather_y(buf, s_sem, r_sem):
+        loop(1, 4, lambda k: send(buf.at[e], buf.at[e], s_sem, r_sem.at[e], y_peer(k)[1]))
+
+    def gather_next(buf, s_sem, r_sem):
+        def step(j):
+            slot = ((zl + 4 - j) % 4) * 4 + y
+            arrived(buf.at[slot], r_sem.at[slot])
+            loop(
+                1, 4,
+                lambda k: send(buf.at[slot], buf.at[slot], s_sem, r_sem.at[slot], y_peer(k)[1]),
+            )
+
+        loop(1, 4, step)
+
+    def gather_done(buf, r_sem):
+        def step(j):
+            def inner(k):
+                slot = ((zl + 4 - j) % 4) * 4 + (y + 4 - k) % 4
+                arrived(buf.at[slot], r_sem.at[slot])
+
+            loop(1, 4, inner)
+
+        loop(0, 4, step)
 
     loads = [
         pltpu.make_async_copy(src, dst, wsem.at[i])
@@ -179,23 +228,15 @@
 
     pl.semaphore_wait(barrier, 25)
 
-    def send_pick(k):
-        q, dev = exp_peer(k)
-        send(gath.at[e], gath.at[e], ssem.at[0], sem_pick.at[e], dev)
-
-    loop(1, 16, send_pick)
-
-    def send_cot(k):
-        q, dev = exp_peer(k)
-        send(cotg.at[e], cotg.at[e], ssem.at[1], sem_cot.at[e], dev)
-
-    loop(1, 16, send_cot)
-
-    def wait_pick(k):
-        q, dev = exp_peer(k)
-        arrived(gath.at[q], sem_pick.at[q])
-
-    loop(1, 16, wait_pick)
+    pick_sems = (ssem.at[0], sem_pick)
+    cot_sems = (ssem.at[1], sem_cot)
+    gather_z(gath, *pick_sems)
+    gather_y(gath, *pick_sems)
+    gather_next(gath, *pick_sems)
+    gather_z(cotg, *cot_sems)
+    gather_done(gath, sem_pick)
+    gather_y(cotg, *cot_sems)
+    gather_next(cotg, *cot_sems)
 
     total = jnp.zeros((128, 128), F32)
     for b in range(16):
@@ -228,25 +269,23 @@
     loads[1].wait()
     for b in range(4):
         cols = slice(b * 512, (b + 1) * 512)
-        part[:, :, cols] = dot(head_out, wout[:, cols]).reshape(16, 8, 512).astype(BF)
-    attr[e] = part[e]
+        rows = dot(head_out, wout[:, cols]).reshape(16, 8, 512).astype(BF)
+        for i in range(16):
+            part[i % 4, i // 4, :, cols] = rows[i]
+    party[y] = part[y]
 
     def send_attn(k):
-        q, dev = exp_peer(k)
-        send(part.at[q], attr.at[e], ssem.at[2], sem_attn.at[e], dev)
-
-    loop(1, 16, send_attn)
-
-    own_slot = ((c * 4 + x) * 2 + h) * 2 + zh
+        q, dev = y_peer(k)
+        send(part.at[q], party.at[y], ssem.at[2], sem_ay.at[y], dev)
+
+    loop(1, 4, send_attn)
+
+    own_slot = (c * 2 + zh) * 8 + xh
 
     def slot_of(core, q, z):
-        return (core * 8 + q) * 2 + z
-
-    def wait_cot(k):
-        q, dev = exp_peer(k)
-        arrived(cotg.at[q], sem_cot.at[q])
-
-    loop(1, 16, wait_cot)
+        return (core * 2 + z) * 8 + q
+
+    gather_done(cotg, sem_cot)
     own_iota = (lax.broadcasted_iota(jnp.int32, (8, 64), 0) + e * 8).astype(F32)
     cot_own = jnp.zeros((8, D), F32)
     for s in range(2):
@@ -300,15 +339,29 @@
     head_t = head_out.astype(F32).T.astype(BF)
     probs_t = soft.T.astype(BF)
 
-    def wait_attn(k):
-        q, dev = exp_peer(k)
-        arrived(attr.at[q], sem_attn.at[q])
-
-    loop(1, 16, wait_attn)
+    def wait_ay(k):
+        q = (y + k) % 4
+        arrived(party.at[q], sem_ay.at[q])
+
+    loop(1, 4, wait_ay)
+
+    def y_sum(z):
+        acc = party[0, z].astype(F32)
+        for b in range(1, 4):
+            acc += party[b, z].astype(F32)
+        return acc
+
+    def send_az(k):
+        q, dev = z_peer(k)
+        zsum[q] = y_sum(q).astype(BF)
+        send(zsum.at[q], partz.at[k - 1], ssem.at[14], sem_az.at[k - 1], dev)
+
+    loop(1, 4, send_az)
+    attn_sum = y_sum(zl)
     own = jnp.concatenate([gath[b, e].astype(F32) for b in range(16)], axis=-1)
-    attn_sum = attr[0].astype(F32)
-    for b in range(1, 16):
-        attn_sum += attr[b].astype(F32)
+    loop(0, 3, lambda k: arrived(partz.at[k], sem_az.at[k]))
+    for b in range(3):
+        attn_sum += partz[b].astype(F32)
     residual = own + attn_sum
     res_scale = lax.rsqrt(jnp.mean(residual * residual, axis=-1, keepdims=True) + EPS)
     fgain = fgain_ref[...]
@@ -345,46 +398,51 @@
         back = dot_nt(grad_gate, wg[cols, :]) + dot_nt(grad_up, wu[cols, :])
         osum[:, 1, :, cols] = back.reshape(32, 8, 512).astype(BF)
 
-    def d1_send(k):
-        q = (xh + k) % 8
-        send(
-            osum.at[pl.ds(slot_of(1 - c, q, 0), 2)], r1.at[pl.ds(2 * q, 2)], ssem.at[5],
-            sem_d1.at[q], sib,
-        )
-
-    loop(1, 9, d1_send)
-
-    def d1_sum(q):
-        arrived(r1.at[pl.ds(2 * q, 2)], sem_d1.at[q])
-        for z in range(2):
-            slot = 2 * q + z
-            s1[slot] = (osum[c * 16 + slot].astype(F32) + r1[slot].astype(F32)).astype(BF)
-
-    def d1_step(k):
-        q, dev = xh_peer(k)
-        d1_sum(q)
-        send(s1.at[pl.ds(2 * q, 2)], r2.at[pl.ds(2 * xh, 2)], ssem.at[6], sem_d2.at[xh], dev)
-
-    loop(1, 8, d1_step)
-    d1_sum(xh)
-    for z in range(2):
-        r2[2 * xh + z] = s1[2 * xh + z]
-
-    def wait_d2(k):
-        q = (xh + k) % 8
-        arrived(r2.at[pl.ds(2 * q, 2)], sem_d2.at[q])
-
-    loop(1, 8, wait_d2)
-
-    def d2_sum(z):
-        acc = r2[z].astype(F32)
-        for b in range(1, 8):
-            acc += r2[2 * b + z].astype(F32)
+    def sum_start(buf, near, s_sem, r_sem, n, me):
+        for z in (1 - zh, zh):
+
+            def step(k):
+                i = z * n + (me + k) % n
+                send(buf.at[(1 - c) * 2 * n + i], near.at[i], s_sem, r_sem.at[i], sib)
+
+            loop(1, n + 1, step)
+
+    def sum_next(buf, near, both, ring, s_sem, near_sem, ring_sem, n, me, peer):
+        for z in (1 - zh, zh):
+
+            def add(q):
+                i = z * n + q
+                arrived(near.at[i], near_sem.at[i])
+                return (buf[c * 2 * n + i].astype(F32) + near[i].astype(F32)).astype(BF)
+
+            def step(k):
+                q, dev = peer(k)
+                i = z * n + q
+                both[i] = add(q)
+                send(both.at[i], ring.at[z * n + me], s_sem, ring_sem.at[z * n + me], dev)
+
+            loop(1, n, step)
+            ring[z * n + me] = add(me)
+
+    def ring_sum(ring, ring_sem, n, me, z):
+        def step(k):
+            i = z * n + (me + k) % n
+            arrived(ring.at[i], ring_sem.at[i])
+
+        loop(1, n, step)
+        acc = ring[z * n].astype(F32)
+        for b in range(1, n):
+            acc += ring[z * n + b].astype(F32)
         return acc
 
-    s3[...] = d2_sum(1 - zh).astype(BF)
-    send(s3, r3, ssem.at[7], sem_d3.at[0], zpart)
-    sums = d2_sum(zh)
+    def sum_far(ring, far_out, far_in, s_sem, ring_sem, far_sem, n, me, dev):
+        far_out[...] = ring_sum(ring, ring_sem, n, me, 1 - zh).astype(BF)
+        send(far_out, far_in, s_sem, far_sem.at[0], dev)
+
+    sum_start(osum, r1, ssem.at[5], sem_d1, 8, xh)
+    sum_next(osum, r1, s1, r2, ssem.at[6], sem_d1, sem_d2, 8, xh, xh_peer)
+    sum_far(r2, s3, r3, ssem.at[7], sem_d2, sem_d3, 8, xh, zpart)
+    sums = ring_sum(r2, sem_d2, 8, xh, zh)
     arrived(r3, sem_d3.at[0])
     own_second = jnp.where(
         jnp.logical_or(jnp.logical_and(e >= 6, e < 12), e >= 14), drop1, drop0
@@ -397,105 +455,97 @@
     grad_norm = grad_in * res_scale - residual * (res_scale * res_scale * res_scale * dot_mean)
     grg[e] = (cot_own + grad_norm).astype(BF)
 
-    def send_gr(k):
-        q, dev = exp_peer(k)
-        send(grg.at[e], grg.at[e], ssem.at[8], sem_gr.at[e], dev)
-
-    loop(1, 16, send_gr)
+    gr_sems = (ssem.at[8], sem_gr)
+    out_sems = (ssem.at[9], sem_out)
+    gather_z(grg, *gr_sems)
+    gather_y(grg, *gr_sems)
     outg[e] = (residual + sums[0]).astype(BF)
-
-    def send_out(k):
-        q, dev = exp_peer(k)
-        send(outg.at[e], outg.at[e], ssem.at[9], sem_out.at[e], dev)
-
-    loop(1, 16, send_out)
-
-    def wait_gr(k):
-        q, dev = exp_peer(k)
-        arrived(grg.at[q], sem_gr.at[q])
-
-    loop(1, 16, wait_gr)
+    gather_next(grg, *gr_sems)
+    gather_z(outg, *out_sems)
+    gather_done(grg, sem_gr)
 
     for b in range(4):
         grmat[32 * b : 32 * b + 32, :] = (
             grg[4 * b : 4 * b + 4].astype(F32).reshape(32, D).astype(BF)
         )
+    for b in range(8):
+        pair = dot(head_t, grmat[:, b * 256 : (b + 1) * 256]).astype(BF)
+        go_part[2 * b] = pair[:, :128]
+        go_part[2 * b + 1] = pair[:, 128:]
+    sum_start(go_part, go_near, ssem.at[10], sem_g1, 4, x)
+    gather_y(outg, *out_sems)
+    gather_next(outg, *out_sems)
     grad_att = dot_nt(grmat[...], wout[...]).astype(BF)
     soft_b = probs32[...]
     grad_probs = dot_nt(grad_att, v_act).astype(BF).astype(F32)
     grad_v = dot(probs_t, grad_att).astype(BF)
+    sum_next(
+        go_part, go_near, go_both, go_ring, ssem.at[11], sem_g1, sem_g2, 4, x, x_peer
+    )
     row_sum = jnp.sum(grad_probs * soft_b, axis=-1, keepdims=True)
     grad_scores = soft_b * (grad_probs - row_sum)
     grad_q = (dot(grad_scores.astype(BF), k_act) * FACTOR).astype(BF)
     grad_k = (dot(grad_scores.T.astype(BF), q_act) * FACTOR).astype(BF)
     stacked = (grad_q, grad_k, grad_v)
-    for j in range(12):
-        f0 = (j % 4) * 512
-        gbuf[j] = dot(norm_t[f0 : f0 + 512, :], stacked[j // 4]).astype(BF)
-    for j in range(4):
-        for b in range(4):
-            c0 = (4 * j + b) * 128
-            gbuf[12 + j, b * 128 : (b + 1) * 128, :] = dot(
-                head_t, grmat[:, c0 : c0 + 128]
+    for j in range(16):
+        row = 384 * j
+        while row < 384 * (j + 1):
+            upto_row = min(384 * (j + 1), (row // D + 1) * D)
+            f0 = row % D
+            gq_part[j, row - 384 * j : upto_row - 384 * j, :] = dot(
+                norm_t[f0 : f0 + upto_row - row, :], stacked[row // D]
             ).astype(BF)
-
-    def g1_send(k):
-        q = (x + k) % 4
-        send(
-            gbuf.at[pl.ds((1 - c) * 8 + 2 * q, 2)], h1.at[pl.ds(2 * q, 2)], ssem.at[10],
-            sem_g1.at[q], sib,
-        )
-
-    loop(1, 5, g1_send)
-
-    def g1_sum(q):
-        arrived(h1.at[pl.ds(2 * q, 2)], sem_g1.at[q])
-        for z in range(2):
-            i = 2 * q + z
-            t1[i] = (gbuf[c * 8 + i].astype(F32) + h1[i].astype(F32)).astype(BF)
-
-    def g1_step(k):
-        q, dev = x_peer(k)
-        g1_sum(q)
-        send(t1.at[pl.ds(2 * q, 2)], h2.at[pl.ds(2 * x, 2)], ssem.at[11], sem_g2.at[x], dev)
-
-    loop(1, 4, g1_step)
-    g1_sum(x)
-    for z in range(2):
-        h2[2 * x + z] = t1[2 * x + z]
-
-    def wait_g2(k):
-        q = (x + k) % 4
-        arrived(h2.at[pl.ds(2 * q, 2)], sem_g2.at[q])
-
-    loop(1, 4, wait_g2)
-
-    def g2_sum(z):
-        acc = h2[z].astype(F32)
-        for b in range(1, 4):
-            acc += h2[2 * b + z].astype(F32)
-        return acc
-
-    t3[...] = g2_sum(1 - zh).astype(BF)
-    send(t3, h3, ssem.at[12], sem_g3.at[0], zsame)
-    seg_sum = g2_sum(zh)
-    arrived(h3, sem_g3.at[0])
-    seg = (c * 4 + x) * 2 + zh
-    seg_z = (c * 4 + x) * 2 + 1 - zh
-    gfin[seg] = (seg_sum + h3[...].astype(F32)).astype(BF)
-
-    def fin(slot, dev):
-        send(gfin.at[slot], gfin.at[slot], ssem.at[13], sem_fin.at[slot], dev)
-
-    fin(seg, zsame)
-    loop(1, 4, lambda k: fin(seg, x_peer(k)[1]))
-    fin(seg, sib)
-
-    def wait_out(k):
-        q, dev = exp_peer(k)
-        arrived(outg.at[q], sem_out.at[q])
-
-    loop(1, 16, wait_out)
+            row = upto_row
+    sum_start(gq_part, gq_near, ssem.at[15], sem_q1, 4, x)
+    sum_far(go_ring, go_out, go_in, ssem.at[12], sem_g2, sem_g3, 4, x, zsame)
+    sum_next(
+        gq_part, gq_near, gq_both, gq_ring, ssem.at[16], sem_q1, sem_q2, 4, x, x_peer
+    )
+    seg = (c * 2 + zh) * 4 + x
+    seg_z = (c * 2 + 1 - zh) * 4 + x
+
+    def sum_own(ring, far_in, fin, ring_sem, far_sem):
+        acc = ring_sum(ring, ring_sem, 4, x, zh)
+        arrived(far_in, far_sem.at[0])
+        fin[seg] = (acc + far_in[...].astype(F32)).astype(BF)
+
+    def fin_send(fin, slot, s_sem, r_sem, dev):
+        send(fin.at[slot], fin.at[slot], s_sem, r_sem.at[slot], dev)
+
+    def fin_first(fin, s_sem, r_sem):
+        fin_send(fin, seg, s_sem, r_sem, zsame)
+        loop(1, 4, lambda k: fin_send(fin, seg, s_sem, r_sem, x_peer(k)[1]))
+        fin_send(fin, seg, s_sem, r_sem, sib)
+
+    def fin_next(fin, s_sem, r_sem):
+        arrived(fin.at[seg_z], r_sem.at[seg_z])
+        loop(1, 4, lambda k: fin_send(fin, seg_z, s_sem, r_sem, x_peer(k)[1]))
+        fin_send(fin, seg_z, s_sem, r_sem, sib)
+
+    def fin_last(fin, s_sem, r_sem, z):
+        def step(k):
+            slot = (c * 2 + z) * 4 + (x + 4 - k) % 4
+            arrived(fin.at[slot], r_sem.at[slot])
+            fin_send(fin, slot, s_sem, r_sem, sib)
+
+        loop(1, 4, step)
+
+    def fin_done(fin, r_sem):
+        def step(k):
+            slot = (1 - c) * 8 + k
+            arrived(fin.at[slot], r_sem.at[slot])
+
+        loop(0, 8, step)
+
+    go_sems = (ssem.at[13], sem_go)
+    gq_sems = (ssem.at[18], sem_gq)
+    sum_own(go_ring, go_in, go_fin, sem_g2, sem_g3)
+    fin_first(go_fin, *go_sems)
+    sum_far(gq_ring, gq_out, gq_in, ssem.at[17], sem_q2, sem_q3, 4, x, zsame)
+    sum_own(gq_ring, gq_in, gq_fin, sem_q2, sem_q3)
+    fin_first(gq_fin, *gq_sems)
+
+    gather_done(outg, sem_out)
     row8 = lax.broadcasted_iota(jnp.int32, (8, 64), 0) + e * 8
     col8 = lax.broadcasted_iota(jnp.int32, (8, 64), 1)
     back_hot = jnp.zeros((8, 128), F32)
@@ -504,27 +554,19 @@
     out_rows = outg[...].astype(F32).reshape(128, D).astype(BF)
     out_ref[...] = dot(back_hot.astype(BF), out_rows).astype(BF)
 
-    arrived(gfin.at[seg_z], sem_fin.at[seg_z])
-    loop(1, 4, lambda k: fin(seg_z, x_peer(k)[1]))
-    fin(seg_z, sib)
-    for z in (zh, 1 - zh):
-
-        def fin_step(k):
-            slot = (c * 4 + (x + 4 - k) % 4) * 2 + z
-            arrived(gfin.at[slot], sem_fin.at[slot])
-            fin(slot, sib)
-
-        loop(1, 4, fin_step)
-
-    def fin_wait(k):
-        slot = (1 - c) * 8 + k
-        arrived(gfin.at[slot], sem_fin.at[slot])
-
-    loop(0, 8, fin_wait)
+    fin_next(go_fin, *go_sems)
+    fin_last(go_fin, *go_sems, zh)
+    fin_last(gq_fin, *gq_sems, zh)
+    fin_next(gq_fin, *gq_sems)
+    fin_last(go_fin, *go_sems, 1 - zh)
+    fin_last(gq_fin, *gq_sems, 1 - zh)
+    fin_done(go_fin, sem_go)
+    fin_done(gq_fin, sem_gq)
 
     sent(gath.at[pl.ds(0, 15)], ssem.at[0])
     sent(cotg.at[pl.ds(0, 15)], ssem.at[1])
-    sent(attr.at[pl.ds(0, 15)], ssem.at[2])
+    sent(party.at[pl.ds(0, 3)], ssem.at[2])
+    sent(partz, ssem.at[14])
     sent(cotr.at[pl.ds(0, 31)], ssem.at[3])
     sent(tokg.at[pl.ds(0, 31)], ssem.at[4])
     sent(r1, ssem.at[5])
@@ -532,10 +574,14 @@
     sent(r3, ssem.at[7])
     sent(grg.at[pl.ds(0, 15)], ssem.at[8])
     sent(outg.at[pl.ds(0, 15)], ssem.at[9])
-    sent(h1, ssem.at[10])
-    sent(h2.at[pl.ds(0, 6)], ssem.at[11])
-    sent(h3, ssem.at[12])
-    sent(gfin.at[pl.ds(0, 15)], ssem.at[13])
+    sent(go_near, ssem.at[10])
+    sent(go_ring.at[pl.ds(0, 6)], ssem.at[11])
+    sent(go_in, ssem.at[12])
+    sent(go_fin.at[pl.ds(0, 15)], ssem.at[13])
+    sent(gq_near, ssem.at[15])
+    sent(gq_ring.at[pl.ds(0, 6)], ssem.at[16])
+    sent(gq_in, ssem.at[17])
+    sent(gq_fin.at[pl.ds(0, 15)], ssem.at[18])
 
 
 def layer(patches, visible, modality, dropped, again, w_qkv, w_out, fgain, wg, wu, wd, cot):
@@ -550,8 +596,10 @@
         pltpu.VMEM((256, D), BF),
         pltpu.VMEM((16, 16, 8, 128), BF),
         pltpu.VMEM((16, 8, D), BF),
-        pltpu.VMEM((16, 8, D), BF),
-        pltpu.VMEM((16, 8, D), BF),
+        pltpu.VMEM((4, 4, 8, D), BF),
+        pltpu.VMEM((4, 4, 8, D), BF),
+        pltpu.VMEM((4, 8, D), BF),
+        pltpu.VMEM((3, 8, D), BF),
         pltpu.VMEM((128, D), BF),
         pltpu.VMEM((D, 128), BF),
         pltpu.VMEM((128, 128), F32),
@@ -568,37 +616,49 @@
         pltpu.VMEM((16, 8, D), BF),
         pltpu.VMEM((16, 8, D), BF),
         pltpu.VMEM((128, D), BF),
-        pltpu.VMEM((16, 512, 128), BF),
-        pltpu.VMEM((8, 512, 128), BF),
-        pltpu.VMEM((8, 512, 128), BF),
-        pltpu.VMEM((8, 512, 128), BF),
-        pltpu.VMEM((512, 128), BF),
-        pltpu.VMEM((512, 128), BF),
+        pltpu.VMEM((16, 128, 128), BF),
+        pltpu.VMEM((8, 128, 128), BF),
+        pltpu.VMEM((8, 128, 128), BF),
+        pltpu.VMEM((8, 128, 128), BF),
+        pltpu.VMEM((128, 128), BF),
+        pltpu.VMEM((128, 128), BF),
+        pltpu.VMEM((16, 384, 128), BF),
+        pltpu.VMEM((8, 384, 128), BF),
+        pltpu.VMEM((8, 384, 128), BF),
+        pltpu.VMEM((8, 384, 128), BF),
+        pltpu.VMEM((384, 128), BF),
+        pltpu.VMEM((384, 128), BF),
         dma((5,)),
-        dma((14,)),
+        dma((19,)),
         dma((16,)),
         dma((16,)),
-        dma((16,)),
+        dma((4,)),
+        dma((3,)),
         dma((32,)),
         dma((32,)),
+        dma((16,)),
+        dma((16,)),
+        dma((1,)),
+        dma((16,)),
+        dma((16,)),
         dma((8,)),
         dma((8,)),
         dma((1,)),
         dma((16,)),
-        dma((16,)),
-        dma((4,)),
-        dma((4,)),
+        dma((8,)),
+        dma((8,)),
         dma((1,)),
         dma((16,)),
     ]
-    out, grads = pl.pallas_call(
+    out, gq, go = pl.pallas_call(
         kernel,
         out_shape=(
             jax.ShapeDtypeStruct((8, D), BF),
-            jax.ShapeDtypeStruct((16, 512, 128), BF),
+            jax.ShapeDtypeStruct((16, 384, 128), BF),
+            jax.ShapeDtypeStruct((16, 128, 128), BF),
         ),
         in_specs=[pl.BlockSpec(memory_space=pltpu.SMEM)] + [vm] * 6 + [anywhere] * 5,
-        out_specs=(vm, vm),
+        out_specs=(vm, vm, vm),
         scratch_shapes=scratch,
         compiler_params=pltpu.CompilerParams(
             collective_id=0, has_side_effects=True, vmem_limit_bytes=56 * 1024 * 1024
@@ -618,8 +678,8 @@
         wu[0],
         wd[0],
     )
-    grad_qkv = grads[:12].reshape(3, D, 128).transpose(1, 0, 2).astype(F32)
-    grad_out = grads[12:].reshape(16, 128, 128).transpose(1, 0, 2).reshape(128, D).astype(F32)
+    grad_qkv = gq.reshape(3, D, 128).transpose(1, 0, 2).astype(F32)
+    grad_out = go.transpose(1, 0, 2).reshape(128, D).astype(F32)
     return out, grad_qkv, grad_out
 
 

time: 153 us -> 126 us (0.82)
  the two profiles are of different devices: /device:TPU:125 before, /device:TPU:1 now
where the time goes in v2:
time: 126 us
  Pallas kernels  120 us (95%)
  other arithmetic  3.43 us (3%)
  local copies, waits for them, and re-layouts  2.26 us (2%)
    pallas_call x1, Pallas kernels, layer(): pl.pallas_call(kernel, out_shape=(jax.ShapeDtypeStruct((8, D), BF), jax.S...  120 us
    convert_element_type x1, other arithmetic, layer(): grad_qkv = gq.reshape(3, D, 128).transpose(1, 0, 2).astype(F32)  3.33 us

profile of v2, /device:TPU:1, one launch (start us, length us, event | category | flops | bytes accessed | tf_op | source)
XLA Modules:
  0.0 126.1 jit_solution(532174614175197863)
XLA Ops:
  0.6 119.7 %layer.1 = (bf16[8,2048]{1,0:T(8,128)(2,1)}, bf16[16,384,128]{2,1,0:T(8,128)(2,1)}, bf16[16,128,128]{2,1,0:T(8,128)(2,1)}) custom-call(s32[2]{0:T(128)} %dropped_ref.1, bf16[2,256,128]{2,1,0:T(8,128)(2,1)} %patches_ref.1, s32[2,64]{1,0:T(2,128)} %visible_ref.1, s32[2,64]{1,0:T(2,128)} %modality_ref.1, f32[16,128]{1,0:T(8,128)} %bitcast.19, ...), custom_call_target="tpu_custom_call" | custom-call | tf_op jit(solution)/shard_map/layer/pallas_call | solution.py:653
  120.3 0.0 copy-start
  120.3 3.3 %convert_bitcast_fusion = f32[2048,3,128]{2,0,1:T(8,128)} fusion(bf16[3,2048,128]{2,1,0:T(8,128)(2,1)} %bitcast.14), kind=kLoop, calls=%fused_computation | loop fusion | flops 786432 | bytes 4718592 | tf_op jit(solution)/shard_map/convert_element_type | solution.py:681
  123.7 0.0 copy-done
  123.7 0.1 convert_bitcast_fusion.1
  123.8 0.3 copy.15
  124.1 0.0 copy-start.1
  124.1 1.3 %copy.16 = f32[128,2048]{1,0:T(8,128)} copy(f32[128,2048]{0,1:T(8,128)S(1)} %bitcast.13) | data formatting | bytes 2097152
  125.4 0.0 copy-done.1
  125.4 0.6 copy.18
Async XLA Ops:
  120.3 3.3 %copy-start = (bf16[16,128,128]{2,1,0:T(8,128)(2,1)S(1)}, bf16[16,128,128]{2,1,0:T(8,128)(2,1)}, u32[]{:S(2)}) copy-start(bf16[16,128,128]{2,1,0:T(8,128)(2,1)} %get-tuple-element.8) | copy-start | bytes 1572868
  124.1 1.3 %copy-start.1 = (bf16[8,2048]{1,0:T(8,128)(2,1)S(1)}, bf16[8,2048]{1,0:T(8,128)(2,1)}, u32[]{:S(2)}) copy-start(bf16[8,2048]{1,0:T(8,128)(2,1)} %get-tuple-element.15) | copy-start | bytes 98308

commit v3 on v2

--- a/solution.py
+++ b/solution.py
@@ -114,10 +114,6 @@
     zpart = (z_row, ((6 - zl) % 4) * 4 + y)
     zsame = (z_row, e)
 
-    def exp_peer(k):
-        q = (e + k) % 16
-        return q, (d, q)
-
     def z_peer(k):
         q = (zl + k) % 4
         return q, (d, q * 4 + y)
@@ -200,7 +196,8 @@
     def greet(dev):
         pl.semaphore_signal(barrier, inc=1, device_id=dev, device_id_type=MESH)
 
-    loop(1, 16, lambda k: greet(exp_peer(k)[1]))
+    loop(1, 4, lambda k: greet(z_peer(k)[1]))
+    loop(1, 4, lambda k: greet(y_peer(k)[1]))
     loop(1, 8, lambda k: greet(xh_peer(k)[1]))
     greet(sib)
     greet(zpart)
@@ -226,7 +223,7 @@
     gath[e] = picked.reshape(16, 8, 128).astype(BF)
     cotg[e] = cot_ref[...]
 
-    pl.semaphore_wait(barrier, 25)
+    pl.semaphore_wait(barrier, 16)
 
     pick_sems = (ssem.at[0], sem_pick)
     cot_sems = (ssem.at[1], sem_cot)
@@ -234,9 +231,9 @@
     gather_y(gath, *pick_sems)
     gather_next(gath, *pick_sems)
     gather_z(cotg, *cot_sems)
-    gather_done(gath, sem_pick)
     gather_y(cotg, *cot_sems)
     gather_next(cotg, *cot_sems)
+    gather_done(gath, sem_pick)
 
     total = jnp.zeros((128, 128), F32)
     for b in range(16):
@@ -332,13 +329,37 @@
 
         loop(0, 16, step)
 
-    spread_first(cotr, ssem.at[3], sem_cotr)
+    h_peer = (d, zl * 4 + y + 1 - 2 * h)
+
+    def share(buf, slot, s_sem, r_sem, devs):
+        src = buf.at[slot]
+        for dev in devs:
+            send(src, src, s_sem, r_sem.at[slot], dev)
+        loop(1, 4, lambda k: send(src, src, s_sem, r_sem.at[slot], x_peer(k)[1]))
+
+    share(cotr, own_slot, ssem.at[3], sem_cotr, (zpart, h_peer, sib))
     for b in range(16):
         cols = slice(b * 128, (b + 1) * 128)
         norm_t[cols, :] = normed[:, cols].astype(F32).T.astype(BF)
     head_t = head_out.astype(F32).T.astype(BF)
     probs_t = soft.T.astype(BF)
 
+    def cot_pass(slot, devs):
+        arrived(cotr.at[slot], sem_cotr.at[slot])
+        share(cotr, slot, ssem.at[3], sem_cotr, devs)
+
+    def cot_rest():
+        for z in (zh, 1 - zh):
+            for other in (0, 1):
+
+                def step(k):
+                    row = (x + 4 - k) % 4 * 2
+                    slot = slot_of(c, row + (h if other == 0 else 1 - h), z)
+                    arrived(cotr.at[slot], sem_cotr.at[slot])
+                    send(cotr.at[slot], cotr.at[slot], ssem.at[3], sem_cotr.at[slot], sib)
+
+                loop(1, 4, step)
+
     def wait_ay(k):
         q = (y + k) % 4
         arrived(party.at[q], sem_ay.at[q])
@@ -357,6 +378,9 @@
         send(zsum.at[q], partz.at[k - 1], ssem.at[14], sem_az.at[k - 1], dev)
 
     loop(1, 4, send_az)
+    cot_pass(slot_of(c, xh, 1 - zh), (h_peer, sib))
+    cot_pass(slot_of(c, x * 2 + 1 - h, zh), (sib,))
+    cot_pass(slot_of(c, x * 2 + 1 - h, 1 - zh), (sib,))
     attn_sum = y_sum(zl)
     own = jnp.concatenate([gath[b, e].astype(F32) for b in range(16)], axis=-1)
     loop(0, 3, lambda k: arrived(partz.at[k], sem_az.at[k]))
@@ -367,9 +391,8 @@
     fgain = fgain_ref[...]
     tokg[own_slot] = (residual * res_scale * fgain).astype(BF)
     spread_first(tokg, ssem.at[4], sem_tok)
-    spread_next(cotr, ssem.at[3], sem_cotr)
     spread_next(tokg, ssem.at[4], sem_tok)
-    spread_last(cotr, ssem.at[3], sem_cotr)
+    cot_rest()
     spread_last(tokg, ssem.at[4], sem_tok)
     spread_done(cotr, sem_cotr)
 
@@ -398,8 +421,8 @@
         back = dot_nt(grad_gate, wg[cols, :]) + dot_nt(grad_up, wu[cols, :])
         osum[:, 1, :, cols] = back.reshape(32, 8, 512).astype(BF)
 
-    def sum_start(buf, near, s_sem, r_sem, n, me):
-        for z in (1 - zh, zh):
+    def sum_start(buf, near, s_sem, r_sem, n, me, halves):
+        for z in halves:
 
             def step(k):
                 i = z * n + (me + k) % n
@@ -407,8 +430,8 @@
 
             loop(1, n + 1, step)
 
-    def sum_next(buf, near, both, ring, s_sem, near_sem, ring_sem, n, me, peer):
-        for z in (1 - zh, zh):
+    def sum_next(buf, near, both, ring, s_sem, near_sem, ring_sem, n, me, peer, halves):
+        for z in halves:
 
             def add(q):
                 i = z * n + q
@@ -435,13 +458,10 @@
             acc += ring[z * n + b].astype(F32)
         return acc
 
-    def sum_far(ring, far_out, far_in, s_sem, ring_sem, far_sem, n, me, dev):
-        far_out[...] = ring_sum(ring, ring_sem, n, me, 1 - zh).astype(BF)
-        send(far_out, far_in, s_sem, far_sem.at[0], dev)
-
-    sum_start(osum, r1, ssem.at[5], sem_d1, 8, xh)
-    sum_next(osum, r1, s1, r2, ssem.at[6], sem_d1, sem_d2, 8, xh, xh_peer)
-    sum_far(r2, s3, r3, ssem.at[7], sem_d2, sem_d3, 8, xh, zpart)
+    sum_start(osum, r1, ssem.at[5], sem_d1, 8, xh, (1 - zh, zh))
+    sum_next(osum, r1, s1, r2, ssem.at[6], sem_d1, sem_d2, 8, xh, xh_peer, (1 - zh, zh))
+    s3[...] = ring_sum(r2, sem_d2, 8, xh, 1 - zh).astype(BF)
+    send(s3, r3, ssem.at[7], sem_d3.at[0], zpart)
     sums = ring_sum(r2, sem_d2, 8, xh, zh)
     arrived(r3, sem_d3.at[0])
     own_second = jnp.where(
@@ -472,7 +492,7 @@
         pair = dot(head_t, grmat[:, b * 256 : (b + 1) * 256]).astype(BF)
         go_part[2 * b] = pair[:, :128]
         go_part[2 * b + 1] = pair[:, 128:]
-    sum_start(go_part, go_near, ssem.at[10], sem_g1, 4, x)
+    sum_start(go_part, go_near, ssem.at[10], sem_g1, 4, x, (0, 1))
     gather_y(outg, *out_sems)
     gather_next(outg, *out_sems)
     grad_att = dot_nt(grmat[...], wout[...]).astype(BF)
@@ -480,7 +500,7 @@
     grad_probs = dot_nt(grad_att, v_act).astype(BF).astype(F32)
     grad_v = dot(probs_t, grad_att).astype(BF)
     sum_next(
-        go_part, go_near, go_both, go_ring, ssem.at[11], sem_g1, sem_g2, 4, x, x_peer
+        go_part, go_near, go_both, go_ring, ssem.at[11], sem_g1, sem_g2, 4, x, x_peer, (0, 1)
     )
     row_sum = jnp.sum(grad_probs * soft_b, axis=-1, keepdims=True)
     grad_scores = soft_b * (grad_probs - row_sum)
@@ -496,31 +516,27 @@
                 norm_t[f0 : f0 + upto_row - row, :], stacked[row // D]
             ).astype(BF)
             row = upto_row
-    sum_start(gq_part, gq_near, ssem.at[15], sem_q1, 4, x)
-    sum_far(go_ring, go_out, go_in, ssem.at[12], sem_g2, sem_g3, 4, x, zsame)
+    sum_start(gq_part, gq_near, ssem.at[15], sem_q1, 4, x, (0, 1))
+
+    def sum_far(ring, far_out, far_in, s_sem, ring_sem, far_sem, z):
+        far_out[z] = ring_sum(ring, ring_sem, 4, x, z).astype(BF)
+        send(far_out.at[z], far_in.at[z], s_sem, far_sem.at[z], zsame)
+
+    for z in range(2):
+        sum_far(go_ring, go_out, go_in, ssem.at[12], sem_g2, sem_g3, z)
     sum_next(
-        gq_part, gq_near, gq_both, gq_ring, ssem.at[16], sem_q1, sem_q2, 4, x, x_peer
+        gq_part, gq_near, gq_both, gq_ring, ssem.at[16], sem_q1, sem_q2, 4, x, x_peer, (0, 1)
     )
-    seg = (c * 2 + zh) * 4 + x
-    seg_z = (c * 2 + 1 - zh) * 4 + x
-
-    def sum_own(ring, far_in, fin, ring_sem, far_sem):
-        acc = ring_sum(ring, ring_sem, 4, x, zh)
-        arrived(far_in, far_sem.at[0])
-        fin[seg] = (acc + far_in[...].astype(F32)).astype(BF)
 
     def fin_send(fin, slot, s_sem, r_sem, dev):
         send(fin.at[slot], fin.at[slot], s_sem, r_sem.at[slot], dev)
 
-    def fin_first(fin, s_sem, r_sem):
-        fin_send(fin, seg, s_sem, r_sem, zsame)
+    def fin_first(far_out, far_in, fin, s_sem, r_sem, far_sem, z):
+        seg = (c * 2 + z) * 4 + x
+        arrived(far_in.at[z], far_sem.at[z])
+        fin[seg] = (far_out[z].astype(F32) + far_in[z].astype(F32)).astype(BF)
         loop(1, 4, lambda k: fin_send(fin, seg, s_sem, r_sem, x_peer(k)[1]))
         fin_send(fin, seg, s_sem, r_sem, sib)
-
-    def fin_next(fin, s_sem, r_sem):
-        arrived(fin.at[seg_z], r_sem.at[seg_z])
-        loop(1, 4, lambda k: fin_send(fin, seg_z, s_sem, r_sem, x_peer(k)[1]))
-        fin_send(fin, seg_z, s_sem, r_sem, sib)
 
     def fin_last(fin, s_sem, r_sem, z):
         def step(k):
@@ -539,11 +555,12 @@
 
     go_sems = (ssem.at[13], sem_go)
     gq_sems = (ssem.at[18], sem_gq)
-    sum_own(go_ring, go_in, go_fin, sem_g2, sem_g3)
-    fin_first(go_fin, *go_sems)
-    sum_far(gq_ring, gq_out, gq_in, ssem.at[17], sem_q2, sem_q3, 4, x, zsame)
-    sum_own(gq_ring, gq_in, gq_fin, sem_q2, sem_q3)
-    fin_first(gq_fin, *gq_sems)
+    for z in range(2):
+        fin_first(go_out, go_in, go_fin, *go_sems, sem_g3, z)
+    for z in range(2):
+        sum_far(gq_ring, gq_out, gq_in, ssem.at[17], sem_q2, sem_q3, z)
+    for z in range(2):
+        fin_first(gq_out, gq_in, gq_fin, *gq_sems, sem_q3, z)
 
     gather_done(outg, sem_out)
     row8 = lax.broadcasted_iota(jnp.int32, (8, 64), 0) + e * 8
@@ -554,12 +571,10 @@
     out_rows = outg[...].astype(F32).reshape(128, D).astype(BF)
     out_ref[...] = dot(back_hot.astype(BF), out_rows).astype(BF)
 
-    fin_next(go_fin, *go_sems)
-    fin_last(go_fin, *go_sems, zh)
-    fin_last(gq_fin, *gq_sems, zh)
-    fin_next(gq_fin, *gq_sems)
-    fin_last(go_fin, *go_sems, 1 - zh)
-    fin_last(gq_fin, *gq_sems, 1 - zh)
+    for z in range(2):
+        fin_last(go_fin, *go_sems, z)
+    for z in range(2):
+        fin_last(gq_fin, *gq_sems, z)
     fin_done(go_fin, sem_go)
     fin_done(gq_fin, sem_gq)
 
@@ -577,11 +592,11 @@
     sent(go_near, ssem.at[10])
     sent(go_ring.at[pl.ds(0, 6)], ssem.at[11])
     sent(go_in, ssem.at[12])
-    sent(go_fin.at[pl.ds(0, 15)], ssem.at[13])
+    sent(go_fin.at[pl.ds(0, 14)], ssem.at[13])
     sent(gq_near, ssem.at[15])
     sent(gq_ring.at[pl.ds(0, 6)], ssem.at[16])
     sent(gq_in, ssem.at[17])
-    sent(gq_fin.at[pl.ds(0, 15)], ssem.at[18])
+    sent(gq_fin.at[pl.ds(0, 14)], ssem.at[18])
 
 
 def layer(patches, visible, modality, dropped, again, w_qkv, w_out, fgain, wg, wu, wd, cot):
@@ -620,14 +635,14 @@
         pltpu.VMEM((8, 128, 128), BF),
         pltpu.VMEM((8, 128, 128), BF),
         pltpu.VMEM((8, 128, 128), BF),
-        pltpu.VMEM((128, 128), BF),
-        pltpu.VMEM((128, 128), BF),
+        pltpu.VMEM((2, 128, 128), BF),
+        pltpu.VMEM((2, 128, 128), BF),
         pltpu.VMEM((16, 384, 128), BF),
         pltpu.VMEM((8, 384, 128), BF),
         pltpu.VMEM((8, 384, 128), BF),
         pltpu.VMEM((8, 384, 128), BF),
-        pltpu.VMEM((384, 128), BF),
-        pltpu.VMEM((384, 128), BF),
+        pltpu.VMEM((2, 384, 128), BF),
+        pltpu.VMEM((2, 384, 128), BF),
         dma((5,)),
         dma((19,)),
         dma((16,)),
@@ -643,11 +658,11 @@
         dma((16,)),
         dma((8,)),
         dma((8,)),
-        dma((1,)),
+        dma((2,)),
         dma((16,)),
         dma((8,)),
         dma((8,)),
-        dma((1,)),
+        dma((2,)),
         dma((16,)),
     ]
     out, gq, go = pl.pallas_call(

time: 126 us -> 122 us (0.968)
  Pallas kernels: 120 us -> 116 us
    pallas_call x1, Pallas kernels: 120 us -> 116 us  [layer(): pl.pallas_call(kernel, out_shape=(jax.ShapeDtypeStruct((8, D), BF), jax.S...]
where the time goes in v3:
time: 122 us
  Pallas kernels  116 us (95%)
  other arithmetic  3.43 us (3%)
  local copies, waits for them, and re-layouts  2.26 us (2%)
    pallas_call x1, Pallas kernels, layer(): pl.pallas_call(kernel, out_shape=(jax.ShapeDtypeStruct((8, D), BF), jax.S...  116 us
    convert_element_type x1, other arithmetic, layer(): grad_qkv = gq.reshape(3, D, 128).transpose(1, 0, 2).astype(F32)  3.33 us

profile of v3, /device:TPU:1, one launch (start us, length us, event | category | flops | bytes accessed | tf_op | source)
XLA Modules:
  0.0 122.2 jit_solution(9530348499995948329)
XLA Ops:
  0.6 115.8 %layer.1 = (bf16[8,2048]{1,0:T(8,128)(2,1)}, bf16[16,384,128]{2,1,0:T(8,128)(2,1)}, bf16[16,128,128]{2,1,0:T(8,128)(2,1)}) custom-call(s32[2]{0:T(128)} %dropped_ref.1, bf16[2,256,128]{2,1,0:T(8,128)(2,1)} %patches_ref.1, s32[2,64]{1,0:T(2,128)} %visible_ref.1, s32[2,64]{1,0:T(2,128)} %modality_ref.1, f32[16,128]{1,0:T(8,128)} %bitcast.19, ...), custom_call_target="tpu_custom_call" | custom-call | tf_op jit(solution)/shard_map/layer/pallas_call | solution.py:668
  116.5 0.0 copy-start
  116.5 3.3 %convert_bitcast_fusion = f32[2048,3,128]{2,0,1:T(8,128)} fusion(bf16[3,2048,128]{2,1,0:T(8,128)(2,1)} %bitcast.14), kind=kLoop, calls=%fused_computation | loop fusion | flops 786432 | bytes 4718592 | tf_op jit(solution)/shard_map/convert_element_type | solution.py:696
  119.8 0.0 copy-done
  119.8 0.1 convert_bitcast_fusion.1
  119.9 0.3 copy.15
  120.3 0.0 copy-start.1
  120.3 1.3 %copy.16 = f32[128,2048]{1,0:T(8,128)} copy(f32[128,2048]{0,1:T(8,128)S(1)} %bitcast.13) | data formatting | bytes 2097152
  121.6 0.0 copy-done.1
  121.6 0.6 copy.18
Async XLA Ops:
  116.5 3.3 %copy-start = (bf16[16,128,128]{2,1,0:T(8,128)(2,1)S(1)}, bf16[16,128,128]{2,1,0:T(8,128)(2,1)}, u32[]{:S(2)}) copy-start(bf16[16,128,128]{2,1,0:T(8,128)(2,1)} %get-tuple-element.8) | copy-start | bytes 1572868
  120.3 1.3 %copy-start.1 = (bf16[8,2048]{1,0:T(8,128)(2,1)S(1)}, bf16[8,2048]{1,0:T(8,128)(2,1)}, u32[]{:S(2)}) copy-start(bf16[8,2048]{1,0:T(8,128)(2,1)} %get-tuple-element.15) | copy-start | bytes 98308

commit v4 on v3

--- a/solution.py
+++ b/solution.py
@@ -38,7 +38,7 @@
     wd_hbm,
     out_ref,
     gq_fin,
-    go_fin,
+    go_ref,
     wqkv,
     wout,
     wg,
@@ -72,6 +72,7 @@
     go_ring,
     go_out,
     go_in,
+    go_fin,
     gq_part,
     gq_near,
     gq_both,
@@ -394,32 +395,37 @@
     spread_next(tokg, ssem.at[4], sem_tok)
     cot_rest()
     spread_last(tokg, ssem.at[4], sem_tok)
+    for i in (2, 3, 4):
+        loads[i].wait()
+
+    def pack_rows(dst, buf, core):
+        for b in range(4):
+            rows = buf[pl.ds(core * 16 + 4 * b, 4)].astype(F32).reshape(32, D)
+            dst[core, 32 * b : 32 * b + 32, :] = rows.astype(BF)
+
+    def experts(core):
+        pack_rows(cmat, cotr, core)
+        pack_rows(tmat, tokg, core)
+        tok = tmat[core]
+        grad_hidden = dot_nt(cmat[core], wd[...])
+        gate = dot(tok, wg[...])
+        up = dot(tok, wu[...])
+        logistic = jax.nn.sigmoid(gate)
+        active = gate * logistic
+        hidden = (active * up).astype(BF)
+        grad_gate = (grad_hidden * up * logistic * (1.0 + gate * (1.0 - logistic))).astype(BF)
+        grad_up = (grad_hidden * active).astype(BF)
+        slots = pl.ds(core * 16, 16)
+        for b in range(4):
+            cols = slice(b * 512, (b + 1) * 512)
+            osum[slots, 0, :, cols] = dot(hidden, wd[:, cols]).reshape(16, 8, 512).astype(BF)
+            back = dot_nt(grad_gate, wg[cols, :]) + dot_nt(grad_up, wu[cols, :])
+            osum[slots, 1, :, cols] = back.reshape(16, 8, 512).astype(BF)
+
+    experts(c)
     spread_done(cotr, sem_cotr)
-
-    def pack_rows(dst, buf):
-        for b in range(8):
-            rows = buf[4 * b : 4 * b + 4].astype(F32).reshape(32, D)
-            dst[32 * b : 32 * b + 32, :] = rows.astype(BF)
-
-    pack_rows(cmat, cotr)
-    loads[2].wait()
-    loads[3].wait()
-    loads[4].wait()
-    grad_hidden = dot_nt(cmat[...], wd[...])
     spread_done(tokg, sem_tok)
-    pack_rows(tmat, tokg)
-    gate = dot(tmat[...], wg[...])
-    up = dot(tmat[...], wu[...])
-    logistic = jax.nn.sigmoid(gate)
-    active = gate * logistic
-    hidden = (active * up).astype(BF)
-    grad_gate = (grad_hidden * up * logistic * (1.0 + gate * (1.0 - logistic))).astype(BF)
-    grad_up = (grad_hidden * active).astype(BF)
-    for b in range(4):
-        cols = slice(b * 512, (b + 1) * 512)
-        osum[:, 0, :, cols] = dot(hidden, wd[:, cols]).reshape(32, 8, 512).astype(BF)
-        back = dot_nt(grad_gate, wg[cols, :]) + dot_nt(grad_up, wu[cols, :])
-        osum[:, 1, :, cols] = back.reshape(32, 8, 512).astype(BF)
+    experts(1 - c)
 
     def sum_start(buf, near, s_sem, r_sem, n, me, halves):
         for z in halves:
@@ -573,9 +579,11 @@
 
     for z in range(2):
         fin_last(go_fin, *go_sems, z)
-    for z in range(2):
-        fin_last(gq_fin, *gq_sems, z)
+    fin_last(gq_fin, *gq_sems, 0)
     fin_done(go_fin, sem_go)
+    for b in range(16):
+        go_ref[:, b * 128 : (b + 1) * 128] = go_fin[b]
+    fin_last(gq_fin, *gq_sems, 1)
     fin_done(gq_fin, sem_gq)
 
     sent(gath.at[pl.ds(0, 15)], ssem.at[0])
@@ -620,8 +628,8 @@
         pltpu.VMEM((128, 128), F32),
         pltpu.VMEM((32, 8, D), BF),
         pltpu.VMEM((32, 8, D), BF),
-        pltpu.VMEM((256, D), BF),
-        pltpu.VMEM((256, D), BF),
+        pltpu.VMEM((2, 128, D), BF),
+        pltpu.VMEM((2, 128, D), BF),
         pltpu.VMEM((32, 2, 8, D), BF),
         pltpu.VMEM((16, 2, 8, D), BF),
         pltpu.VMEM((16, 2, 8, D), BF),
@@ -637,6 +645,7 @@
         pltpu.VMEM((8, 128, 128), BF),
         pltpu.VMEM((2, 128, 128), BF),
         pltpu.VMEM((2, 128, 128), BF),
+        pltpu.VMEM((16, 128, 128), BF),
         pltpu.VMEM((16, 384, 128), BF),
         pltpu.VMEM((8, 384, 128), BF),
         pltpu.VMEM((8, 384, 128), BF),
@@ -670,7 +679,7 @@
         out_shape=(
             jax.ShapeDtypeStruct((8, D), BF),
             jax.ShapeDtypeStruct((16, 384, 128), BF),
-            jax.ShapeDtypeStruct((16, 128, 128), BF),
+            jax.ShapeDtypeStruct((128, D), BF),
         ),
         in_specs=[pl.BlockSpec(memory_space=pltpu.SMEM)] + [vm] * 6 + [anywhere] * 5,
         out_specs=(vm, vm, vm),
@@ -694,7 +703,7 @@
         wd[0],
     )
     grad_qkv = gq.reshape(3, D, 128).transpose(1, 0, 2).astype(F32)
-    grad_out = go.transpose(1, 0, 2).reshape(128, D).astype(F32)
+    grad_out = go.astype(F32)
     return out, grad_qkv, grad_out
 
 

time: 122 us -> 121 us (level)
  local copies, waits for them, and re-layouts: 2.26 us -> 0.62 us
    unnamed x6 -> x5, local copies, waits for them, and re-layouts: 1.93 us -> 0.62 us
where the time goes in v4:
time: 121 us
  Pallas kernels  116 us (96%)
  other arithmetic  4.41 us (4%)
    pallas_call x1, Pallas kernels, layer(): pl.pallas_call(kernel, out_shape=(jax.ShapeDtypeStruct((8, D), BF), jax.S...  116 us
    convert_element_type x1, other arithmetic, layer(): grad_qkv = gq.reshape(3, D, 128).transpose(1, 0, 2).astype(F32)  3.33 us

profile of v4, /device:TPU:1, one launch (start us, length us, event | category | flops | bytes accessed | tf_op | source)
XLA Modules:
  0.0 121.2 jit_solution(10854081140541510015)
XLA Ops:
  0.6 115.6 %layer.1 = (bf16[8,2048]{1,0:T(8,128)(2,1)}, bf16[16,384,128]{2,1,0:T(8,128)(2,1)}, bf16[128,2048]{1,0:T(8,128)(2,1)}) custom-call(s32[2]{0:T(128)} %dropped_ref.1, bf16[2,256,128]{2,1,0:T(8,128)(2,1)} %patches_ref.1, s32[2,64]{1,0:T(2,128)} %visible_ref.1, s32[2,64]{1,0:T(2,128)} %modality_ref.1, f32[16,128]{1,0:T(8,128)} %bitcast.15, f32[1,2048]{1,0:T(1,128)} %bitcast.16, ...), custom_call_target="tpu_custom_call" | custom-call | tf_op jit(solution)/shard_map/layer/pallas_call | solution.py:677
  116.2 0.0 copy-start
  116.2 3.3 %convert_bitcast_fusion = f32[2048,3,128]{2,0,1:T(8,128)} fusion(bf16[3,2048,128]{2,1,0:T(8,128)(2,1)} %bitcast.10), kind=kLoop, calls=%fused_computation | loop fusion | flops 786432 | bytes 4718592 | tf_op jit(solution)/shard_map/convert_element_type | solution.py:705
  119.6 0.0 copy-start.1
  119.6 0.0 copy-done
  119.6 1.1 convert_element_type.15
  120.6 0.0 copy-done.1
  120.6 0.6 copy.16
Async XLA Ops:
  116.2 3.3 %copy-start = (bf16[128,2048]{1,0:T(8,128)(2,1)S(1)}, bf16[128,2048]{1,0:T(8,128)(2,1)}, u32[]{:S(2)}) copy-start(bf16[128,2048]{1,0:T(8,128)(2,1)} %get-tuple-element.8) | copy-start | bytes 1572868
  119.6 1.1 copy-start.1

commit v5 on v4

--- a/solution.py
+++ b/solution.py
@@ -563,11 +563,6 @@
     gq_sems = (ssem.at[18], sem_gq)
     for z in range(2):
         fin_first(go_out, go_in, go_fin, *go_sems, sem_g3, z)
-    for z in range(2):
-        sum_far(gq_ring, gq_out, gq_in, ssem.at[17], sem_q2, sem_q3, z)
-    for z in range(2):
-        fin_first(gq_out, gq_in, gq_fin, *gq_sems, sem_q3, z)
-
     gather_done(outg, sem_out)
     row8 = lax.broadcasted_iota(jnp.int32, (8, 64), 0) + e * 8
     col8 = lax.broadcasted_iota(jnp.int32, (8, 64), 1)
@@ -578,11 +573,16 @@
     out_ref[...] = dot(back_hot.astype(BF), out_rows).astype(BF)
 
     for z in range(2):
+        sum_far(gq_ring, gq_out, gq_in, ssem.at[17], sem_q2, sem_q3, z)
+    for z in range(2):
         fin_last(go_fin, *go_sems, z)
-    fin_last(gq_fin, *gq_sems, 0)
     fin_done(go_fin, sem_go)
     for b in range(16):
         go_ref[:, b * 128 : (b + 1) * 128] = go_fin[b]
+    for z in range(2):
+        fin_first(gq_out, gq_in, gq_fin, *gq_sems, sem_q3, z)
+
+    fin_last(gq_fin, *gq_sems, 0)
     fin_last(gq_fin, *gq_sems, 1)
     fin_done(gq_fin, sem_gq)
 

time: 121 us -> 122 us (level)
  no operation moved by 1% of the time
where the time goes in v5:
time: 122 us
  Pallas kernels  116 us (95%)
  other arithmetic  4.41 us (4%)
    pallas_call x1, Pallas kernels, layer(): pl.pallas_call(kernel, out_shape=(jax.ShapeDtypeStruct((8, D), BF), jax.S...  116 us
    convert_element_type x1, other arithmetic, layer(): grad_qkv = gq.reshape(3, D, 128).transpose(1, 0, 2).astype(F32)  3.33 us

profile of v5, /device:TPU:1, one launch (start us, length us, event | category | flops | bytes accessed | tf_op | source)
XLA Modules:
  0.0 122.0 jit_solution(9766230362050997243)
XLA Ops:
  0.6 116.3 %layer.1 = (bf16[8,2048]{1,0:T(8,128)(2,1)}, bf16[16,384,128]{2,1,0:T(8,128)(2,1)}, bf16[128,2048]{1,0:T(8,128)(2,1)}) custom-call(s32[2]{0:T(128)} %dropped_ref.1, bf16[2,256,128]{2,1,0:T(8,128)(2,1)} %patches_ref.1, s32[2,64]{1,0:T(2,128)} %visible_ref.1, s32[2,64]{1,0:T(2,128)} %modality_ref.1, f32[16,128]{1,0:T(8,128)} %bitcast.15, f32[1,2048]{1,0:T(1,128)} %bitcast.16, ...), custom_call_target="tpu_custom_call" | custom-call | tf_op jit(solution)/shard_map/layer/pallas_call | solution.py:677
  117.0 0.0 copy-start
  117.0 3.3 %convert_bitcast_fusion = f32[2048,3,128]{2,0,1:T(8,128)} fusion(bf16[3,2048,128]{2,1,0:T(8,128)(2,1)} %bitcast.10), kind=kLoop, calls=%fused_computation | loop fusion | flops 786432 | bytes 4718592 | tf_op jit(solution)/shard_map/convert_element_type | solution.py:705
  120.3 0.0 copy-start.1
  120.3 0.0 copy-done
  120.3 1.1 convert_element_type.15
  121.4 0.0 copy-done.1
  121.4 0.6 copy.16
Async XLA Ops:
  117.0 3.3 %copy-start = (bf16[128,2048]{1,0:T(8,128)(2,1)S(1)}, bf16[128,2048]{1,0:T(8,128)(2,1)}, u32[]{:S(2)}) copy-start(bf16[128,2048]{1,0:T(8,128)(2,1)} %get-tuple-element.8) | copy-start | bytes 1572868
  120.3 1.1 copy-start.1
